TPU v7x, 32 devices: a whole 2x2x4 slice. The times are simulated.
32 devices in a mesh: expert: 8 (over z, y), head: 4 (over x, core).
Axes of the slice: x: 2, y: 2, z: 4, core: 2. Of those that a mesh axis runs over, the one named last changes fastest.
Arguments:
- tokens: bfloat16 [32768, 512], P(('expert', 'head')), may hold values from -6 to 6
- segment_ids: int32 [32768], P('expert'), may hold values from 0 to 1023, never falling along the last dimension, each value on 1 to 64 neighbouring positions
- task_ids: int32 [1024], replicated, may hold values from 0 to 63
- task_table: int32 [64, 2], replicated, may hold values from 0 to 7, as said below
- weight_qkv: float32 [3, 512, 512], P(None, 'expert', 'head'), may hold values from -0.25 to 0.25
- weight_out: float32 [512, 512], P('head', 'expert'), may hold values from -1 to 1
- gain_one: float32 [512], P('expert'), may hold values from 0.5 to 1.5
- gain_two: float32 [512], P('expert'), may hold values from 0.5 to 1.5
- weight_router: float32 [512, 8], P('expert'), may hold values from -0.1875 to 0.1875
- weight_in: float32 [8, 512, 2048], P('expert', 'head'), may hold values from -0.25 to 0.25
- weight_hidden: float32 [8, 2048, 512], P('expert', 'head'), may hold values from -0.1875 to 0.1875
- cotangent: bfloat16 [32768, 512], P(('expert', 'head')), may hold values from -6 to 6
Outputs:
- output: bfloat16 [32768, 512], P(('expert', 'head'))
- grad_tokens: float32 [32768, 512], P(('expert', 'head'))
- grad_qkv: float32 [3, 512, 512], P(None, 'expert', 'head')
- grad_out: float32 [512, 512], P('head', 'expert')
- grad_gain_one: float32 [512], P('expert')
- grad_gain_two: float32 [512], P('expert')
- grad_router: float32 [512, 8], P('expert')
- grad_in: float32 [8, 512, 2048], P('expert', 'head')
- grad_hidden: float32 [8, 2048, 512], P('expert', 'head')
Inputs may be any that keep to these rules, and one draw needn't show every extreme that they name: `task_table`: each row names two different experts; every expert stands in the first column of some row.
All inputs are finite; a program needn't handle non-finite values.
Results may differ from a plain program's by a relative error of at most 0.024.
Values may be sent and summed in bfloat16 or wider, within the bound.
No kernel may reach another device: no remote copies, remote signals or barrier semaphores. Data moves between devices by JAX's collectives and lax.ppermute only.
A program may use at most 192 MiB of HBM per device.

v0:
```python
import jax
import jax.numpy as jnp
from jax import lax
from jax.sharding import PartitionSpec as P

HDIM = 64
PACK = 1024


EPSILON = 1e-05
NEGATIVE = -1e30


def norm_forward(values, gain_vector):
    centered = values - jnp.mean(values, axis=-1, keepdims=True)
    inverse = lax.rsqrt(jnp.mean(centered * centered, axis=-1, keepdims=True) + EPSILON)
    scaled = centered * inverse
    return (scaled * gain_vector.astype(jnp.float32), scaled, inverse)


def norm_backward(grad_normed, scaled, inverse, gain_vector):
    grad_scaled = grad_normed * gain_vector.astype(jnp.float32)
    grad_values = inverse * (
        grad_scaled
        - jnp.mean(grad_scaled, axis=-1, keepdims=True)
        - scaled * jnp.mean(grad_scaled * scaled, axis=-1, keepdims=True)
    )
    return (grad_values, jnp.sum(grad_normed * scaled, axis=0))


def masked_scores(queries, keys_block, segments):
    score_scale = queries.shape[-1] ** (-0.5)
    scores = (
        jnp.einsum("qhd,khd->hqk", queries, keys_block, preferred_element_type=jnp.float32)
        * score_scale
    )
    same_segment = segments[:, None] == segments[None, :]
    return jnp.where(same_segment[None], scores, NEGATIVE)


def attend_block(operands):
    queries, keys_block, values_block, segments = operands
    scores = masked_scores(queries, keys_block, segments)
    row_peak = jnp.max(scores, axis=-1, keepdims=True)
    exponent = jnp.exp(scores - row_peak)
    row_total = jnp.sum(exponent, axis=-1, keepdims=True)
    softmax_low = (exponent / row_total).astype(jnp.bfloat16)
    attended = jnp.einsum(
        "hqk,khd->qhd", softmax_low, values_block, preferred_element_type=jnp.float32
    )
    return (attended.astype(jnp.bfloat16), (row_peak + jnp.log(row_total))[..., 0])


def attend_back(operands):
    queries, keys_block, values_block, segments, log_total, grad_attended = operands
    score_scale = queries.shape[-1] ** (-0.5)
    scores = masked_scores(queries, keys_block, segments)
    softmax_values = jnp.exp(scores - log_total[..., None])
    softmax_low = softmax_values.astype(jnp.bfloat16)
    grad_softmax = jnp.einsum(
        "qhd,khd->hqk", grad_attended, values_block, preferred_element_type=jnp.float32
    )
    grad_values = jnp.einsum(
        "hqk,qhd->khd", softmax_low, grad_attended, preferred_element_type=jnp.float32
    )
    row_delta = jnp.sum(softmax_values * grad_softmax, axis=-1, keepdims=True)
    grad_scores = (softmax_values * (grad_softmax - row_delta)).astype(jnp.bfloat16)
    grad_queries = (
        jnp.einsum("hqk,khd->qhd", grad_scores, keys_block, preferred_element_type=jnp.float32)
        * score_scale
    )
    grad_keys = (
        jnp.einsum("hqk,qhd->khd", grad_scores, queries, preferred_element_type=jnp.float32)
        * score_scale
    )
    return jnp.stack([grad_queries, grad_keys, grad_values]).astype(jnp.bfloat16)


def gelu_tanh(values):
    return jax.nn.gelu(values, approximate=True)


def per_device(
    tokens,
    segment_ids,
    task_ids,
    task_table,
    weight_qkv,
    weight_out,
    gain_one,
    gain_two,
    weight_router,
    weight_in,
    weight_hidden,
    cotangent,
):
    bfloat = jnp.bfloat16
    single = jnp.float32
    expert_count = lax.axis_size("expert")
    head_index = lax.axis_index("head")
    row_count, model_width = tokens.shape
    params = (
        lax.all_gather(weight_qkv.astype(bfloat), "expert", axis=1, tiled=True),
        lax.all_gather(weight_out.astype(bfloat), "expert", axis=1, tiled=True),
        lax.all_gather(gain_one.astype(bfloat), "expert", axis=0, tiled=True),
        lax.all_gather(gain_two.astype(bfloat), "expert", axis=0, tiled=True),
        lax.all_gather(weight_router.astype(bfloat), "expert", axis=0, tiled=True),
    )
    qkv_weight, out_weight, gain_first, gain_second, router_weight = params
    expert_weights = (
        lax.all_gather(weight_in.astype(bfloat), "head", axis=1, tiled=True),
        lax.all_gather(weight_hidden.astype(bfloat), "head", axis=1, tiled=True),
    )
    expert_in = expert_weights[0][0]
    expert_hidden = expert_weights[1][0]
    cap = 4 * row_count // expert_count
    token_values = tokens.astype(single)
    normed_one, scaled_one, inverse_one = norm_forward(token_values, gain_first)
    normed_low = normed_one.astype(bfloat)
    group_rows = lax.all_gather(normed_low, "head", axis=0, tiled=True)
    group_count = group_rows.shape[0]
    head_width = qkv_weight.shape[2]
    heads_here = head_width // HDIM
    pack_count = group_count // PACK
    projected = jnp.einsum(
        "gd,cde->cge", group_rows, qkv_weight, preferred_element_type=single
    ).astype(bfloat)
    blocks = projected.reshape(3, pack_count, PACK, heads_here, HDIM)
    segment_packs = segment_ids.reshape(pack_count, PACK)
    attended, log_total = lax.map(attend_block, (blocks[0], blocks[1], blocks[2], segment_packs))
    attn_low = attended.reshape(group_count, head_width)
    residual = token_values + lax.psum_scatter(
        jnp.dot(attn_low, out_weight, preferred_element_type=single),
        "head",
        scatter_dimension=0,
        tiled=True,
    )
    normed_two, scaled_two, inverse_two = norm_forward(residual, gain_second)
    two_low = normed_two.astype(bfloat)
    own_segments = lax.dynamic_slice_in_dim(segment_ids, head_index * row_count, row_count)
    chosen = task_table[task_ids[own_segments]]
    expert_range = jnp.arange(expert_count, dtype=jnp.int32)
    pair_marks = chosen[:, :, None] == expert_range
    logits = jnp.dot(two_low, router_weight, preferred_element_type=single)
    picked = jnp.sum(jnp.where(pair_marks, logits[:, None, :], 0.0), axis=-1)
    gate_weights = jax.nn.softmax(picked, axis=-1)
    flat_choice = chosen.reshape(-1)
    expert_marks = (flat_choice[:, None] == expert_range).astype(jnp.int32)
    running = jnp.cumsum(expert_marks, axis=0)
    slot_index = jnp.sum((running - 1) * expert_marks, axis=1)
    destination = jnp.where(slot_index < cap, flat_choice * cap + slot_index, expert_count * cap)
    send_rows = (
        jnp.zeros((expert_count * cap + 1, model_width), bfloat)
        .at[destination]
        .set(jnp.repeat(two_low, 2, axis=0))
    )
    send_rows = send_rows[:-1].reshape(expert_count, cap, model_width)
    received = lax.all_to_all(send_rows, "expert", split_axis=0, concat_axis=0, tiled=True)
    flat_in = received.reshape(-1, model_width)
    hidden_pre = jnp.dot(flat_in, expert_in, preferred_element_type=single)
    activated, gelu_pullback = jax.vjp(gelu_tanh, hidden_pre)
    act_low = activated.astype(bfloat)
    results = jnp.dot(act_low, expert_hidden, preferred_element_type=single).astype(bfloat)
    returned = lax.all_to_all(
        results.reshape(expert_count, cap, model_width),
        "expert",
        split_axis=0,
        concat_axis=0,
        tiled=True,
    )
    zero_row = jnp.zeros((1, model_width), bfloat)
    back_pairs = (
        jnp.concatenate([returned.reshape(-1, model_width), zero_row])[destination]
        .astype(single)
        .reshape(row_count, 2, model_width)
    )
    output = (residual + jnp.sum(gate_weights[:, :, None] * back_pairs, axis=1)).astype(bfloat)
    grad_top = cotangent.astype(single)
    grad_pairs = (
        (gate_weights[:, :, None] * grad_top[:, None, :]).reshape(-1, model_width).astype(bfloat)
    )
    send_grad = (
        jnp.zeros((expert_count * cap + 1, model_width), bfloat).at[destination].set(grad_pairs)
    )
    send_grad = send_grad[:-1].reshape(expert_count, cap, model_width)
    grad_gates = jnp.sum(back_pairs * grad_top[:, None, :], axis=-1)
    grad_picked = gate_weights * (
        grad_gates - jnp.sum(gate_weights * grad_gates, axis=-1, keepdims=True)
    )
    grad_logits = jnp.sum(jnp.where(pair_marks, grad_picked[:, :, None], 0.0), axis=1)
    grad_results = lax.all_to_all(send_grad, "expert", split_axis=0, concat_axis=0, tiled=True)
    flat_grad = grad_results.reshape(-1, model_width)
    grad_act = jnp.einsum("rd,fd->rf", flat_grad, expert_hidden, preferred_element_type=single)
    grad_hidden_local = jnp.einsum("rf,rd->fd", act_low, flat_grad, preferred_element_type=single)
    grad_pre = gelu_pullback(grad_act)[0].astype(bfloat)
    grad_in_local = jnp.einsum("rd,rf->df", flat_in, grad_pre, preferred_element_type=single)
    grad_rows = jnp.einsum("rf,df->rd", grad_pre, expert_in, preferred_element_type=single).astype(
        bfloat
    )
    grad_back = lax.all_to_all(
        grad_rows.reshape(expert_count, cap, model_width),
        "expert",
        split_axis=0,
        concat_axis=0,
        tiled=True,
    )
    grad_copies = jnp.concatenate([grad_back.reshape(-1, model_width), zero_row])[
        destination
    ].astype(single)
    grad_copies = jnp.sum(grad_copies.reshape(row_count, 2, model_width), axis=1)
    grad_normed_two = grad_copies + jnp.einsum(
        "re,de->rd", grad_logits, router_weight.astype(single)
    )
    grad_router_local = jnp.einsum("rd,re->de", two_low, grad_logits, preferred_element_type=single)
    grad_residual_two, grad_gain_two_local = norm_backward(
        grad_normed_two, scaled_two, inverse_two, gain_second
    )
    grad_residual = grad_top + grad_residual_two
    grad_group = lax.all_gather(grad_residual.astype(bfloat), "head", axis=0, tiled=True)
    grad_out_local = jnp.einsum("gk,gd->kd", attn_low, grad_group, preferred_element_type=single)
    grad_heads = jnp.einsum(
        "gd,kd->gk", grad_group, out_weight, preferred_element_type=single
    ).astype(bfloat)
    grad_blocks = lax.map(
        attend_back,
        (
            blocks[0],
            blocks[1],
            blocks[2],
            segment_packs,
            log_total,
            grad_heads.reshape(pack_count, PACK, heads_here, HDIM),
        ),
    )
    grad_projected = jnp.moveaxis(grad_blocks, 1, 0).reshape(3, group_count, head_width)
    grad_qkv_local = jnp.einsum(
        "gd,cge->cde", group_rows, grad_projected, preferred_element_type=single
    )
    grad_normed_one = lax.psum_scatter(
        jnp.einsum("cge,cde->gd", grad_projected, qkv_weight, preferred_element_type=single).astype(
            jnp.bfloat16
        ),
        "head",
        scatter_dimension=0,
        tiled=True,
    ).astype(jnp.float32)
    grad_residual_one, grad_gain_one_local = norm_backward(
        grad_normed_one, scaled_one, inverse_one, gain_first
    )
    grad_tokens = grad_residual + grad_residual_one
    small_totals = (
        lax.psum(grad_gain_one_local.astype(jnp.bfloat16), "head").astype(jnp.float32),
        lax.psum(grad_gain_two_local.astype(jnp.bfloat16), "head").astype(jnp.float32),
        lax.psum(grad_router_local.astype(jnp.bfloat16), "head").astype(jnp.float32),
    )
    param_totals = (
        lax.psum_scatter(
            grad_qkv_local.astype(jnp.bfloat16), "expert", scatter_dimension=1, tiled=True
        ).astype(jnp.float32),
        lax.psum_scatter(
            grad_out_local.astype(jnp.bfloat16), "expert", scatter_dimension=1, tiled=True
        ).astype(jnp.float32),
        lax.psum_scatter(
            small_totals[0].astype(jnp.bfloat16), "expert", scatter_dimension=0, tiled=True
        ).astype(jnp.float32),
        lax.psum_scatter(
            small_totals[1].astype(jnp.bfloat16), "expert", scatter_dimension=0, tiled=True
        ).astype(jnp.float32),
        lax.psum_scatter(
            small_totals[2].astype(jnp.bfloat16), "expert", scatter_dimension=0, tiled=True
        ).astype(jnp.float32),
    )
    expert_totals = (
        lax.psum_scatter(
            grad_in_local[None].astype(jnp.bfloat16), "head", scatter_dimension=1, tiled=True
        ).astype(jnp.float32),
        lax.psum_scatter(
            grad_hidden_local[None].astype(jnp.bfloat16), "head", scatter_dimension=1, tiled=True
        ).astype(jnp.float32),
    )
    return (
        output,
        grad_tokens,
        param_totals[0],
        param_totals[1],
        param_totals[2],
        param_totals[3],
        param_totals[4],
        expert_totals[0],
        expert_totals[1],
    )


def solution(mesh):
    placed = (
        P(("expert", "head"), None),
        P("expert"),
        P(),
        P(),
        P(None, "expert", "head"),
        P("head", "expert"),
        P("expert"),
        P("expert"),
        P("expert", None),
        P("expert", "head", None),
        P("expert", "head", None),
        P(("expert", "head"), None),
    )
    return jax.shard_map(
        per_device,
        mesh=mesh,
        in_specs=placed,
        out_specs=(
            P(("expert", "head"), None),
            P(("expert", "head"), None),
            P(None, "expert", "head"),
            P("head", "expert"),
            P("expert"),
            P("expert"),
            P("expert", None),
            P("expert", "head", None),
            P("expert", "head", None),
        ),
        check_vma=False,
    )
```

profile of v0, /device:TPU:0, one launch (start us, length us, event | category | flops | bytes accessed | tf_op | source)
XLA Modules:
  0.0 1127.1 jit_solution(6034810762022828142)
XLA Ops:
  11.1 23.1 %all-reduce.8 = (bf16[512]{0:T(512)(128)(2,1)S(1)}, bf16[512]{0:T(512)(128)(2,1)S(1)}) all-reduce(bf16[512]{0:T(512)(128)(2,1)S(1)} %dynamic-update-slice, bf16[512]{0:T(512)(128)(2,1)S(1)} %dynamic-update-slice.1), channel_id=1, replica_groups=mesh['expert'=8,'head'=4] {'expert'}, use_global_device_ids=true, to_apply=%add.2 | all-reduce | flops 1024 | bytes 4096
  40.8 30.5 %all_gather.30 = bf16[128,512]{0,1:T(8,128)(2,1)S(1)} all-gather(bf16[128,64]{0,1:T(8,128)(2,1)S(1)} %convert_element_type.188), channel_id=1, replica_groups=mesh['expert'=8,'head'=4] {'expert'}, dimensions={1}, use_global_device_ids=true | all-gather | bytes 147456 | tf_op jit(solution)/shard_map/all_gather | solution.py:104
  71.3 30.9 %all_gather.29 = bf16[3,512,128]{2,1,0:T(8,128)(2,1)S(1)} all-gather(bf16[3,64,128]{2,1,0:T(8,128)(2,1)S(1)} %convert_element_type.185), channel_id=1, replica_groups=mesh['expert'=8,'head'=4] {'expert'}, dimensions={1}, use_global_device_ids=true | all-gather | bytes 442368 | tf_op jit(solution)/shard_map/all_gather | solution.py:103
  102.3 4.7 fusion.61
  118.4 5.1 reshape.515
  123.5 4.6 copy.119
  128.1 35.6 %while.22 = (s32[]{:T(128)}, bf16[4,1024,2,64]{1,3,2,0:T(8,128)(2,1)S(1)}, f32[4,2,1024]{2,1,0:T(2,128)}, bf16[4,1024,2,64]{1,3,2,0:T(8,128)(2,1)}, s32[4,1024]{...) while((s32[]{:T(128)}, ...), condition=%wide.region_5.6_spmd, body=%wide.region_2.5_spmd.sunk | while | flops 563214336 | bytes 30489176 | solution.py:130
  166.0 4.5 fusion.107
  171.3 4.5 gather_fusion
  182.7 56.9 %reduce-scatter.9.cloned.1.call-done = f32[1024,512]{1,0:T(8,128)} async-done(((f32[4096,512]{1,0:T(8,128)}), f32[1024,512]{1,0:T(8,128)}) %reduce-scatter.9.cloned.1.call-update) | async-done | bytes 2097168 | tf_op jit(solution)/shard_map/reduce_scatter | solution.py:132
  249.8 12.6 %scatter_custom_fusion = bf16[4097,512]{1,0:T(8,128)(2,1)} fusion(s32[2048]{0:T(1024)S(1)} %bitcast.208, bf16[2048,512]{1,0:T(8,128)(2,1)} %reshape.480, bf16[]{:T(256)} %constant.52.clone.1), kind=kCustom, calls=%fused_computation.110 | custom fusion | bytes 4195840 | tf_op jit(solution)/shard_map/scatter | solution.py:155
  262.4 4.4 slice.46
  266.8 5.6 all-to-all-start
  274.8 109.3 %all-gather = bf16[8,64,8]{1,2,0:T(8,128)(2,1)S(1)} all-gather(bf16[1,64,8]{1,2,0:T(8,128)(2,1)S(1)} %convert_bitcast_fusion), channel_id=1, replica_groups=mesh['expert'=8,'head'=4] {'expert'}, dimensions={0}, use_global_device_ids=true | all-gather | bytes 9216 | tf_op jit(solution)/shard_map/all_gather | solution.py:107
  387.2 6.4 mul.243
  395.8 13.6 %scatter_custom_fusion.1 = bf16[4097,512]{1,0:T(8,128)(2,1)} fusion(s32[2048]{0:T(1024)S(1)} %bitcast.209, bf16[]{:T(256)} %constant.52.clone.1, f32[2048,512]{1,0:T(8,128)} %mul.243, f32[2048]{0:T(1024)S(1)} %div.57), kind=kCustom, calls=%fused_computation.108 | custom fusion | flops 2097152 | bytes 8397826 | tf_op jit(solution)/shard_map/scatter | solution.py:183
  409.4 4.5 slice.47
  413.9 4.7 all-to-all-start.2
  419.6 24.0 %multiply_convert_fusion.1 = (bf16[4096,2048]{1,0:T(8,128)(2,1)}, f32[4096,2048]{1,0:T(8,128)}) fusion(bf16[4096,512]{1,0:T(8,128)(2,1)} %bitcast.29, bf16[1,512,2048]{2,1,0:T(8,128)(2,1)} %all-gather.8.cloned.1.call-done), kind=kOutput, calls=%fused_computation.79 | convolution fusion | flops 8665432064 | bytes 56623104 | tf_op jit(solution)/shard_map/dot_general | solution.py:160
  444.3 14.4 %convolution_convert_fusion.1 = bf16[4096,512]{1,0:T(8,128)(2,1)} fusion(bf16[4096,2048]{1,0:T(8,128)(2,1)} %get-tuple-element.271, bf16[1,2048,512]{2,1,0:T(8,128)(2,1)} %all-gather.10.cloned.1.call-done), kind=kOutput, calls=%fused_computation.82 | convolution fusion | flops 8592031744 | bytes 23068672 | tf_op jit(solution)/shard_map/dot_general | solution.py:163
  458.7 48.7 %all-to-all-done.2 = bf16[8,512,512]{2,1,0:T(8,128)(2,1)} async-done(((bf16[8,512,512]{2,1,0:T(8,128)(2,1)}), bf16[8,512,512]{2,1,0:T(8,128)(2,1)}, u32[]{:S(2)}, u32[]{:S(2)}) %all-to-all-start.2) | async-done | bytes 4194336 | tf_op jit(solution)/shard_map/all_to_all | solution.py:191
  507.4 5.0 all-to-all-start.1
  512.4 31.8 %fusion.60 = bf16[4096,2048]{1,0:T(8,128)(2,1)} fusion(f32[4096,2048]{1,0:T(8,128)} %get-tuple-element.272, bf16[4096,512]{1,0:T(8,128)(2,1)} %bitcast.35, bf16[1,2048,512]{2,1,0:T(8,128)(2,1)S(1)} %copy-done.55), kind=kOutput, calls=%fused_computation.78 | convolution fusion | flops 8757706752 | bytes 56623104 | tf_op jit(solution)/shard_map/rd,fd->rf/dot_general | solution.py:193
  544.2 13.9 %convolution_convert_fusion = bf16[4096,512]{1,0:T(8,128)(2,1)} fusion(bf16[4096,2048]{1,0:T(8,128)(2,1)} %fusion.60, bf16[1,512,2048]{2,1,0:T(8,128)(2,1)S(1)} %copy-done.54), kind=kOutput, calls=%fused_computation.81 | convolution fusion | flops 8592031744 | bytes 23068672 | tf_op jit(solution)/shard_map/rf,df->rd/dot_general | solution.py:197
  558.1 46.6 %all-to-all-done.1 = bf16[8,512,512]{2,1,0:T(8,128)(2,1)} async-done(((bf16[8,512,512]{2,1,0:T(8,128)(2,1)}), bf16[8,512,512]{2,1,0:T(8,128)(2,1)}, u32[]{:S(2)}, u32[]{:S(2)}) %all-to-all-start.1) | async-done | bytes 4194336 | tf_op jit(solution)/shard_map/all_to_all | solution.py:164
  604.7 4.7 all-to-all-start.3
  611.0 4.4 concatenate.14
  615.4 10.3 gather_fusion.2
  629.8 11.3 %multiply_reduce_fusion.1 = (f32[1024,2]{1,0:T(8,128)S(1)}, f32[1024,512]{1,0:T(8,128)}) fusion(f32[1024,2,512]{2,1,0:T(2,128)} %reshape.442, f32[1024,512]{1,0:T(8,128)} %convert_element_type.201, f32[1024,2]{1,0:T(8,128)} %copy-done.19), kind=kLoop, calls=%fused_computation.89 | loop fusion | flops 3667968 | bytes 8404992 | tf_op jit(solution)/shard_map/reduce_sum | solution.py:186
  641.3 60.6 %all-to-all-done.3 = bf16[8,512,512]{2,1,0:T(8,128)(2,1)} async-done(((bf16[8,512,512]{2,1,0:T(8,128)(2,1)}), bf16[8,512,512]{2,1,0:T(8,128)(2,1)}, u32[]{:S(2)}, u32[]{:S(2)}) %all-to-all-start.3) | async-done | bytes 4194336 | tf_op jit(solution)/shard_map/all_to_all | solution.py:200
  701.9 4.4 concatenate.15
  706.3 10.3 gather_fusion.3
  716.6 4.4 reshape.443
  721.1 8.6 reduce_sum.191
  735.5 14.9 %fusion.66 = bf16[1,2048,512]{2,1,0:T(8,128)(2,1)} fusion(bf16[4096,2048]{1,0:T(8,128)(2,1)} %get-tuple-element.271, bf16[4096,512]{1,0:T(8,128)(2,1)} %bitcast.35), kind=kOutput, calls=%fused_computation.98 | convolution fusion | flops 8590983168 | bytes 23068672 | tf_op jit(solution)/shard_map/rf,rd->fd/dot_general | solution.py:194
  750.5 14.9 %fusion.65 = bf16[1,512,2048]{2,1,0:T(8,128)(2,1)} fusion(bf16[4096,512]{1,0:T(8,128)(2,1)} %bitcast.29, bf16[4096,2048]{1,0:T(8,128)(2,1)} %fusion.60), kind=kOutput, calls=%fused_computation.97 | convolution fusion | flops 8590983168 | bytes 23068672 | tf_op jit(solution)/shard_map/rd,rf->df/dot_general | solution.py:196
  773.6 6.0 copy.132
  779.6 63.2 %while.23 = (s32[]{:T(128)}, bf16[4,3,1024,2,64]{2,4,3,1,0:T(8,128)(2,1)}, bf16[4,1024,2,64]{1,3,2,0:T(8,128)(2,1)S(1)}, s32[4,1024]{1,0:T(4,128)}, bf16[4,1024,...) while((s32[]{:T(128)}, ...), condition=%wide.region_26.27_spmd, body=%wide.region_24.26_spmd.sunk | while | flops 1377695744 | bytes 75569808 | solution.py:224
  842.8 4.6 convolution_convert_fusion.6
  847.4 4.3 copy.134
  855.8 5.1 fusion.94
  862.1 5.4 bitcast_convert_fusion
  872.7 28.1 %reduce-scatter.19.cloned.1.call-done = bf16[64,8]{1,0:T(8,128)(2,1)} async-done(((bf16[512,8]{1,0:T(8,128)(2,1)}), bf16[64,8]{1,0:T(8,128)(2,1)}) %reduce-scatter.19.cloned.1.call-update) | async-done | bytes 1040
  901.6 62.8 %reduce-scatter.13.cloned.1.call-done = bf16[128,64]{0,1:T(8,128)(2,1)} async-done(((bf16[128,512]{0,1:T(8,128)(2,1)}), bf16[128,64]{0,1:T(8,128)(2,1)}) %reduce-scatter.13.cloned.1.call-update) | async-done | bytes 16400 | tf_op jit(solution)/shard_map/reduce_scatter | solution.py:260
  965.7 73.7 %all-reduce.12.cloned.1.call-done = bf16[3,512,128]{2,0,1:T(4,128)(2,1)} async-done(((bf16[3,512,128]{2,0,1:T(4,128)(2,1)}), bf16[3,512,128]{2,0,1:T(4,128)(2,1)}) %all-reduce.12.cloned.1.call-update) | async-done | bytes 393232
  1040.9 44.9 %reduce-scatter.11.cloned.1.call-done = bf16[1024,512]{1,0:T(8,128)(2,1)} async-done(((bf16[4096,512]{1,0:T(8,128)(2,1)}), bf16[1024,512]{1,0:T(8,128)(2,1)}) %reduce-scatter.11.cloned.1.call-update) | async-done | bytes 1048592 | tf_op jit(solution)/shard_map/reduce_scatter | solution.py:239
  1088.4 21.4 %all-reduce.7 = (bf16[512]{0:T(512)(128)(2,1)S(1)}, bf16[512]{0:T(512)(128)(2,1)S(1)}) all-reduce(bf16[512]{0:T(512)(128)(2,1)S(1)} %get-tuple-element.216, bf16[512]{0:T(512)(128)(2,1)S(1)} %get-tuple-element.212), channel_id=6, replica_groups=mesh['expert'=8,'head'=4] {'expert'}, use_global_device_ids=true, to_apply=%region_34.35.clone | all-reduce | flops 1024 | bytes 4096
  1109.9 5.9 all-reduce.9
  (306 shorter events, 188.8 us)
Async XLA Ops:
  7.2 164.1 %copy-start = (s32[1024]{0:T(1024)S(1)}, s32[1024]{0:T(1024)}, u32[]{:S(2)}) copy-start(s32[1024]{0:T(1024)} %param.18) | copy-start | bytes 12292
  7.2 33.5 %copy-start.35 = (f32[3,64,128]{2,1,0:T(8,128)S(1)}, f32[3,64,128]{2,1,0:T(8,128)}, u32[]{:S(2)}) copy-start(f32[3,64,128]{2,1,0:T(8,128)} %param.20) | copy-start | bytes 294916
  7.2 33.6 %copy-start.51 = (s32[4096]{0:T(1024)S(1)}, s32[4096]{0:T(1024)}, u32[]{:S(2)}) copy-start(s32[4096]{0:T(1024)} %param.17) | copy-start | bytes 49156
  7.2 33.6 %copy-start.50 = (f32[128,64]{0,1:T(8,128)S(1)}, f32[128,64]{0,1:T(8,128)}, u32[]{:S(2)}) copy-start(f32[128,64]{0,1:T(8,128)} %param.21) | copy-start | bytes 98308
  7.2 95.1 %all-gather.6.cloned.1.call-start = ((), (), s32[]{:S(2)}) async-start(), calls=%async_computation.10 | async-start | bytes 5242880 | tf_op jit(solution)/shard_map/all_gather | solution.py:120
  40.7 199.0 %reduce-scatter.9.cloned.1.call-start = ((), (), s32[]{:S(2)}) async-start(), calls=%async_computation.11 | async-start | bytes 10485760 | tf_op jit(solution)/shard_map/reduce_scatter | solution.py:132
  71.3 93.6 %copy-start.21 = (bf16[128,512]{0,1:T(8,128)(2,1)}, bf16[128,512]{0,1:T(8,128)(2,1)S(1)}, u32[]{:S(2)}) copy-start(bf16[128,512]{0,1:T(8,128)(2,1)S(1)} %all_gather.30) | copy-start | bytes 393220
  118.4 9.7 copy-start.24
  175.8 63.8 %copy-start.4 = (bf16[1024,512]{1,0:T(8,128)(2,1)S(1)}, bf16[1024,512]{1,0:T(8,128)(2,1)}, u32[]{:S(2)}) copy-start(bf16[1024,512]{1,0:T(8,128)(2,1)} %param.16) | copy-start | bytes 3145732
  179.4 62.6 %copy-start.46 = (f32[512]{0:T(512)}, f32[512]{0:T(512)S(1)}, u32[]{:S(2)}) copy-start(f32[512]{0:T(512)S(1)} %convert_element_type.190) | copy-start | bytes 6148
  243.2 150.4 %copy-start.6 = (bf16[1024,512]{1,0:T(8,128)(2,1)}, bf16[1024,512]{1,0:T(8,128)(2,1)S(1)}, u32[]{:S(2)}) copy-start(bf16[1024,512]{1,0:T(8,128)(2,1)S(1)} %multiply_convert_fusion.4) | copy-start | bytes 3145732
  266.8 117.4 %copy-start.14 = (bf16[1024,512]{1,0:T(8,128)(2,1)S(1)}, bf16[1024,512]{1,0:T(8,128)(2,1)}, u32[]{:S(2)}) copy-start(bf16[1024,512]{1,0:T(8,128)(2,1)} %param.27) | copy-start | bytes 3145732
  266.8 147.1 %all-to-all-start = ((bf16[8,512,512]{2,1,0:T(8,128)(2,1)}), bf16[8,512,512]{2,1,0:T(8,128)(2,1)}, u32[]{:S(2)}, u32[]{:S(2)}) async-start(bf16[8,512,512]{2,1,0:T(8,128)(2,1)} %bitcast.198), calls=%async_computation.1 | async-start | bytes 8388608 | tf_op jit(solution)/shard_map/all_to_all | solution.py:158
  272.4 147.1 %all-gather.8.cloned.1.call-start = ((), (), s32[]{:S(2)}) async-start(), calls=%async_computation.12 | async-start | bytes 2621440 | tf_op jit(solution)/shard_map/all_gather | solution.py:111
  274.8 119.3 %copy-start.38 = (s32[1024,2]{0,1:T(2,128)}, s32[1024,2]{0,1:T(2,128)S(1)}, u32[]{:S(2)}) copy-start(s32[1024,2]{0,1:T(2,128)S(1)} %copy.122) | copy-start | bytes 24580
  384.2 9.5 copy-start.36
  394.1 15.2 %copy-start.31 = (f32[1024]{0:T(1024)}, f32[1024]{0:T(1024)S(1)}, u32[]{:S(2)}) copy-start(f32[1024]{0:T(1024)S(1)} %reduce_max.18) | copy-start | bytes 12292
  395.5 13.8 %copy-start.19 = (f32[1024,2]{1,0:T(8,128)}, f32[1024,2]{1,0:T(8,128)S(1)}, u32[]{:S(2)}) copy-start(f32[1024,2]{1,0:T(8,128)S(1)} %copy.124) | copy-start | bytes 24580
  413.9 93.5 %all-to-all-start.2 = ((bf16[8,512,512]{2,1,0:T(8,128)(2,1)}), bf16[8,512,512]{2,1,0:T(8,128)(2,1)}, u32[]{:S(2)}, u32[]{:S(2)}) async-start(bf16[8,512,512]{2,1,0:T(8,128)(2,1)} %bitcast.199), calls=%async_computation.3 | async-start | bytes 8388608 | tf_op jit(solution)/shard_map/all_to_all | solution.py:191
  418.6 25.7 %all-gather.10.cloned.1.call-start = ((), (), s32[]{:S(2)}) async-start(), calls=%async_computation.13 | async-start | bytes 2621440 | tf_op jit(solution)/shard_map/all_gather | solution.py:112
  507.4 97.3 %all-to-all-start.1 = ((bf16[8,512,512]{2,1,0:T(8,128)(2,1)}), bf16[8,512,512]{2,1,0:T(8,128)(2,1)}, u32[]{:S(2)}, u32[]{:S(2)}) async-start(bf16[8,512,512]{2,1,0:T(8,128)(2,1)} %bitcast.203), calls=%async_computation.2 | async-start | bytes 8388608 | tf_op jit(solution)/shard_map/all_to_all | solution.py:164
  512.4 31.9 %copy-start.54 = (bf16[1,512,2048]{2,1,0:T(8,128)(2,1)S(1)}, bf16[1,512,2048]{2,1,0:T(8,128)(2,1)}, u32[]{:S(2)}) copy-start(bf16[1,512,2048]{2,1,0:T(8,128)(2,1)} %all-gather.8.cloned.1.call-done) | copy-start | bytes 6291460
  604.7 97.3 %all-to-all-start.3 = ((bf16[8,512,512]{2,1,0:T(8,128)(2,1)}), bf16[8,512,512]{2,1,0:T(8,128)(2,1)}, u32[]{:S(2)}, u32[]{:S(2)}) async-start(bf16[8,512,512]{2,1,0:T(8,128)(2,1)} %bitcast.202), calls=%async_computation.4 | async-start | bytes 8388608 | tf_op jit(solution)/shard_map/all_to_all | solution.py:200
  609.4 158.9 %all-gather.12.cloned.1.call-start = ((), (), s32[]{:S(2)}) async-start(), calls=%async_computation.14 | async-start | bytes 5242880 | tf_op jit(solution)/shard_map/all_gather | solution.py:219
  629.8 11.5 %copy-start.27 = (f32[1024,2]{0,1:T(2,128)S(1)}, f32[1024,2]{0,1:T(2,128)}, u32[]{:S(2)}) copy-start(f32[1024,2]{0,1:T(2,128)} %copy-done.26) | copy-start | bytes 24580
  629.8 11.5 %copy-start.32 = (f32[1024]{0:T(1024)S(1)}, f32[1024]{0:T(1024)}, u32[]{:S(2)}) copy-start(f32[1024]{0:T(1024)} %copy-done.31) | copy-start | bytes 12292
  629.8 11.5 %copy-start.43 = (f32[1024]{0:T(1024)S(1)}, f32[1024]{0:T(1024)}, u32[]{:S(2)}) copy-start(f32[1024]{0:T(1024)} %copy-done.42) | copy-start | bytes 12292
  629.8 11.6 %copy-start.39 = (s32[1024,2]{0,1:T(2,128)S(1)}, s32[1024,2]{0,1:T(2,128)}, u32[]{:S(2)}) copy-start(s32[1024,2]{0,1:T(2,128)} %copy-done.38) | copy-start | bytes 24580
  721.1 8.7 copy-start.3
  721.1 8.7 copy-start.30
  721.1 8.6 copy-start.37
  721.1 8.6 copy-start.41
  721.1 8.6 copy-start.47
  735.5 132.9 %reduce-scatter.17.cloned.1.call-start = ((), (), s32[]{:S(2)}) async-start(), calls=%async_computation.18 | async-start | bytes 2621440 | tf_op jit(solution)/shard_map/reduce_scatter | solution.py:277
  750.4 15.1 %copy-start.7 = (bf16[1024,512]{1,0:T(8,128)(2,1)S(1)}, bf16[1024,512]{1,0:T(8,128)(2,1)}, u32[]{:S(2)}) copy-start(bf16[1024,512]{1,0:T(8,128)(2,1)} %copy-done.6) | copy-start | bytes 3145732
  750.4 17.8 %copy-start.22 = (bf16[128,512]{0,1:T(8,128)(2,1)S(1)}, bf16[128,512]{0,1:T(8,128)(2,1)}, u32[]{:S(2)}) copy-start(bf16[128,512]{0,1:T(8,128)(2,1)} %copy-done.21) | copy-start | bytes 393220
  750.4 120.1 %reduce-scatter.15.cloned.1.call-start = ((), (), s32[]{:S(2)}) async-start(), calls=%async_computation.17 | async-start | bytes 2621440 | tf_op jit(solution)/shard_map/reduce_scatter | solution.py:274
  765.5 135.3 %reduce-scatter.19.cloned.1.call-start = ((), (), s32[]{:S(2)}) async-start(), calls=%async_computation.19 | async-start | bytes 147456
  766.6 197.8 %reduce-scatter.13.cloned.1.call-start = ((), (), s32[]{:S(2)}) async-start(), calls=%async_computation.16 | async-start | bytes 147456 | tf_op jit(solution)/shard_map/reduce_scatter | solution.py:260
  779.6 63.2 %copy-start.13 = (bf16[16,8,4,1024]{3,1,2,0:T(8,128)(2,1)S(1)}, bf16[16,8,4,1024]{3,1,2,0:T(8,128)(2,1)}, u32[]{:S(2)}) copy-start(bf16[16,8,4,1024]{3,1,2,0:T(8,128)(2,1)} %copy-done.12) | copy-start | bytes 3145732
  855.8 183.7 %all-reduce.12.cloned.1.call-start = ((), (), s32[]{:S(2)}) async-start(), calls=%async_computation.20 | async-start | bytes 1048576
  862.0 223.8 %reduce-scatter.11.cloned.1.call-start = ((), (), s32[]{:S(2)}) async-start(), calls=%async_computation.15 | async-start | bytes 5242880 | tf_op jit(solution)/shard_map/reduce_scatter | solution.py:239
  867.4 218.3 %copy-start.5 = (bf16[1024,512]{1,0:T(8,128)(2,1)S(1)}, bf16[1024,512]{1,0:T(8,128)(2,1)}, u32[]{:S(2)}) copy-start(bf16[1024,512]{1,0:T(8,128)(2,1)} %param.16) | copy-start | bytes 3145732
  867.4 218.3 %copy-start.34 = (f32[1024]{0:T(1024)S(1)}, f32[1024]{0:T(1024)}, u32[]{:S(2)}) copy-start(f32[1024]{0:T(1024)} %copy-done.33) | copy-start | bytes 12292
  867.4 218.3 %copy-start.45 = (f32[1024]{0:T(1024)S(1)}, f32[1024]{0:T(1024)}, u32[]{:S(2)}) copy-start(f32[1024]{0:T(1024)} %copy-done.44) | copy-start | bytes 12292
  867.4 218.3 %copy-start.49 = (f32[512]{0:T(512)S(1)}, f32[512]{0:T(512)}, u32[]{:S(2)}) copy-start(f32[512]{0:T(512)} %copy-done.48) | copy-start | bytes 6148
  867.5 250.0 %copy-start.16 = (f32[1024,512]{1,0:T(8,128)S(1)}, f32[1024,512]{1,0:T(8,128)}, u32[]{:S(2)}) copy-start(f32[1024,512]{1,0:T(8,128)} %get-tuple-element.258) | copy-start | bytes 6291460
  1040.3 80.1 %copy-start.1 = (s32[1024]{0:T(1024)S(1)}, s32[1024]{0:T(1024)}, u32[]{:S(2)}) copy-start(s32[1024]{0:T(1024)} %param.18) | copy-start | bytes 12292
  (26 other events, 106.9 us)
Sparse Core Ops, SparseCore 0:
  40.8 31.7 all-gather.5
  170.6 68.9 reduce-scatter.8
  275.5 23.0 all-gather.7
  421.3 22.9 all-gather.9
  735.6 32.5 all-gather.11
  770.8 31.4 reduce-scatter.16
  804.8 31.4 reduce-scatter.14
  839.9 60.8 reduce-scatter.18
  904.5 59.8 reduce-scatter.12
  968.1 71.3 all-reduce.11
  1041.9 43.7 reduce-scatter.10
where the time goes:
time: 1130 us
  waiting for transfers between devices  425 us (38%)
  blocking collectives  221 us (20%)
  matrix products  208 us (18%)
  local copies, waits for them, and re-layouts  139 us (12%)
  other arithmetic  97.1 us (9%)
  starting transfers between devices  20.4 us (2%)
  between operations  16.5 us (1%)
    all_gather x1, blocking collectives, per_device(): lax.all_gather(weight_router.astype(bfloat), 'expert', axis=0, tiled=True)  109 us
    unnamed x13, waiting for transfers between devices  102 us
    reduce_scatter x1, waiting for transfers between devices, per_device(): lax.psum_scatter(grad_out_local.astype(jnp.bfloat16), 'expert', scatter_d...  62.8 us
    all_to_all x1, waiting for transfers between devices, per_device(): lax.all_to_all(grad_rows.reshape(expert_count, cap, model_width), 'expert...  60.6 us
    reduce_scatter x1, waiting for transfers between devices, per_device(): lax.psum_scatter(jnp.dot(attn_low, out_weight, preferred_element_type=sin...  56.9 us
    all_to_all x1, waiting for transfers between devices, per_device(): lax.all_to_all(send_grad, 'expert', split_axis=0, concat_axis=0, tiled=True)  48.7 us
    all_to_all x1, waiting for transfers between devices, per_device(): lax.all_to_all(results.reshape(expert_count, cap, model_width), 'expert',...  46.6 us
    reduce_scatter x1, waiting for transfers between devices, per_device(): lax.psum_scatter(jnp.einsum('cge,cde->gd', grad_projected, qkv_weight, pr...  44.9 us
  transfers between devices with their start and end apart: 15, of which 10 were waited for; matrix products, arithmetic and copies ran while one was open for 26% of the time, Pallas kernels for 0%

commit v1 on v0

v1 whole, which is shorter than its diff:
```python
import jax
import jax.numpy as jnp
from jax import lax
from jax.experimental import pallas as pl
from jax.experimental.pallas import tpu as pltpu
from jax.sharding import PartitionSpec as P

HDIM = 64
PACK = 1024
SPAN = 64
BLOCK = 128
WINDOW = BLOCK + 2 * SPAN
CHUNK = 256
LANES = 128

EPSILON = 1e-05
NEGATIVE = -1e30

bfloat = jnp.bfloat16
single = jnp.float32
VMEM_LIMIT = 56 * 1024 * 1024


def dot_nn(a, b):
    return lax.dot_general(a, b, (((1,), (0,)), ((), ())), preferred_element_type=single)


def dot_nt(a, b):
    return lax.dot_general(a, b, (((1,), (1,)), ((), ())), preferred_element_type=single)


def dot_tn(a, b):
    return lax.dot_general(a, b, (((0,), (0,)), ((), ())), preferred_element_type=single)


def normalise(values):
    centered = values - jnp.mean(values, axis=-1, keepdims=True)
    inverse = lax.rsqrt(jnp.mean(centered * centered, axis=-1, keepdims=True) + EPSILON)
    return centered * inverse, inverse


def norm_pull(grad_normed, scaled, inverse, gain):
    weighted = grad_normed * gain
    return inverse * (
        weighted
        - jnp.mean(weighted, axis=-1, keepdims=True)
        - scaled * jnp.mean(weighted * scaled, axis=-1, keepdims=True)
    )


def split_heads(pair, first_half):
    zero = jnp.zeros_like(pair)
    return jnp.concatenate(
        [jnp.where(first_half, pair, zero), jnp.where(first_half, zero, pair)], axis=0
    )


def window_start(block, rows):
    return pl.multiple_of(jnp.clip(block * BLOCK - SPAN, 0, rows - WINDOW), SPAN)


def forward_kernel(
    tok, wqkv, wot, gain1, gain2, router, segc, segw, first, second,
    proj, attn, res, two, stat, gate,
):
    rows, width = tok.shape

    def project(step, carry):
        at = pl.ds(pl.multiple_of(step * CHUNK, CHUNK), CHUNK)
        scaled, _ = normalise(tok[at, :].astype(single))
        low = (scaled * gain1[...]).astype(bfloat)
        for part in range(3):
            proj[part, at, :] = dot_nn(low, wqkv[part]).astype(bfloat)
        return carry

    lax.fori_loop(0, rows // CHUNK, project, 0)
    lane = lax.broadcasted_iota(jnp.int32, (BLOCK, LANES), 1)
    first_half = lane < HDIM
    expert = lax.broadcasted_iota(jnp.int32, (router.shape[0], BLOCK), 0)

    def attend(block, carry):
        q_at = pl.ds(pl.multiple_of(block * BLOCK, BLOCK), BLOCK)
        k_at = pl.ds(window_start(block, rows), WINDOW)
        same = (segc[q_at, :] == segw[pl.ds(block, 1), :])[None]
        totals = jnp.zeros((BLOCK, LANES), single)
        for pair in range(width // LANES):
            cols = slice(pair * LANES, (pair + 1) * LANES)
            queries = split_heads(proj[0, q_at, cols] * HDIM**-0.5, first_half)
            scores = dot_nt(queries, proj[1, k_at, cols]).reshape(2, BLOCK, WINDOW)
            scores = jnp.where(same, scores, NEGATIVE)
            peak = jnp.max(scores, axis=-1, keepdims=True)
            exponent = jnp.exp(scores - peak)
            total = jnp.sum(exponent, axis=-1, keepdims=True)
            probs = (exponent * (1.0 / total)).astype(bfloat).reshape(2 * BLOCK, WINDOW)
            out = dot_nn(probs, proj[2, k_at, cols])
            attn[q_at, cols] = jnp.where(first_half, out[:BLOCK], out[BLOCK:]).astype(bfloat)
            log_total = peak + jnp.log(total)
            for half in range(2):
                totals = jnp.where(lane == 2 * pair + half, log_total[half], totals)
        stat[q_at, :] = totals
        residual = tok[q_at, :].astype(single) + dot_nt(attn[q_at, :], wot[...])
        res[q_at, :] = residual
        scaled, _ = normalise(residual)
        low = (scaled * gain2[...]).astype(bfloat)
        two[q_at, :] = low
        logits = dot_nt(router[...], low)
        mark0 = first[:, q_at] == expert
        mark1 = second[:, q_at] == expert
        logit0 = jnp.sum(jnp.where(mark0, logits, 0.0), axis=0, keepdims=True)
        logit1 = jnp.sum(jnp.where(mark1, logits, 0.0), axis=0, keepdims=True)
        top = jnp.maximum(logit0, logit1)
        part0, part1 = jnp.exp(logit0 - top), jnp.exp(logit1 - top)
        scale = 1.0 / (part0 + part1)
        gate[:, q_at] = jnp.where(mark0, part0 * scale, jnp.where(mark1, part1 * scale, 0.0))
        return carry

    lax.fori_loop(0, rows // BLOCK, attend, 0)


def backward_kernel(
    tok, cot, res, two, proj, attn, stat, wqkv, wot, gain1, gain2, router, segc, segw,
    gate, inner, copies,
    grad_tok, grad_w, grad_gain1, grad_gain2, grad_router,
    grad_res, grad_attn, grad_heads, grad_proj, grad_key, grad_value, normed,
):
    rows, width = tok.shape
    weights = gate[...]
    inner_products = inner[...]
    grad_logits = weights * (
        inner_products - jnp.sum(weights * inner_products, axis=0, keepdims=True)
    )
    logits_high = grad_logits.astype(bfloat)
    logits_low = (grad_logits - logits_high.astype(single)).astype(bfloat)
    grad_logits = jnp.concatenate([logits_high, logits_low], axis=0)
    router_twice = jnp.concatenate([router[...], router[...]], axis=0)
    count = router.shape[0]
    routed = dot_nn(grad_logits, two[...])
    grad_router[...] = routed[:count] + routed[count:]
    grad_gain1[...] = jnp.zeros_like(grad_gain1)
    grad_gain2[...] = jnp.zeros_like(grad_gain2)
    grad_key[...] = jnp.zeros_like(grad_key)
    grad_value[...] = jnp.zeros_like(grad_value)
    for step in range(rows // CHUNK):
        at = slice(step * CHUNK, (step + 1) * CHUNK)
        scaled, inverse = normalise(res[at, :])
        grad_normed = copies[at, :].astype(single) + dot_tn(grad_logits[:, at], router_twice)
        grad_gain2[...] += jnp.sum(grad_normed * scaled, axis=0, keepdims=True)
        grad_row = cot[at, :].astype(single) + norm_pull(grad_normed, scaled, inverse, gain2[...])
        grad_res[at, :] = grad_row
        low = grad_row.astype(bfloat)
        grad_attn[at, :] = low
        grad_heads[at, :] = dot_nn(low, wot[...]).astype(bfloat)
    grad_w[3] = dot_tn(grad_attn[...], attn[...]).astype(bfloat)
    lane = lax.broadcasted_iota(jnp.int32, (BLOCK, LANES), 1)
    first_half = lane < HDIM

    def attend(block, carry):
        q_at = pl.ds(pl.multiple_of(block * BLOCK, BLOCK), BLOCK)
        k_at = pl.ds(window_start(block, rows), WINDOW)
        same = (segc[q_at, :] == segw[pl.ds(block, 1), :])[None]
        totals = stat[q_at, :]
        for pair in range(width // LANES):
            cols = slice(pair * LANES, (pair + 1) * LANES)
            queries = split_heads(proj[0, q_at, cols] * HDIM**-0.5, first_half)
            keys_block = proj[1, k_at, cols]
            scores = dot_nt(queries, keys_block).reshape(2, BLOCK, WINDOW)
            scores = jnp.where(same, scores, NEGATIVE)
            log_total = jnp.stack([totals[:, 2 * pair : 2 * pair + 1], totals[:, 2 * pair + 1 : 2 * pair + 2]])
            probs = jnp.exp(scores - log_total).reshape(2 * BLOCK, WINDOW)
            heads = split_heads(grad_heads[q_at, cols], first_half)
            grad_probs = dot_nt(heads, proj[2, k_at, cols])
            delta = jnp.sum(probs * grad_probs, axis=-1, keepdims=True)
            grad_scores = (probs * (grad_probs - delta)).astype(bfloat)
            grad_query = dot_nn(grad_scores, keys_block) * HDIM**-0.5
            grad_proj[0, q_at, cols] = jnp.where(
                first_half, grad_query[:BLOCK], grad_query[BLOCK:]
            ).astype(bfloat)
            grad_key[k_at, cols] += dot_tn(grad_scores, queries)
            grad_value[k_at, cols] += dot_tn(probs.astype(bfloat), heads)
        return carry

    lax.fori_loop(0, rows // BLOCK, attend, 0)
    for step in range(rows // CHUNK):
        at = slice(step * CHUNK, (step + 1) * CHUNK)
        grad_proj[1, at, :] = grad_key[at, :].astype(bfloat)
        grad_proj[2, at, :] = grad_value[at, :].astype(bfloat)
        grad_normed = dot_nt(grad_proj[0, at, :], wqkv[0])
        for part in (1, 2):
            grad_normed += dot_nt(grad_proj[part, at, :], wqkv[part])
        scaled, inverse = normalise(tok[at, :].astype(single))
        normed[at, :] = (scaled * gain1[...]).astype(bfloat)
        grad_gain1[...] += jnp.sum(grad_normed * scaled, axis=0, keepdims=True)
        grad_tok[at, :] = grad_res[at, :] + norm_pull(grad_normed, scaled, inverse, gain1[...])
    for part in range(3):
        grad_w[part] = dot_tn(normed[...], grad_proj[part]).astype(bfloat)


def whole_call(kernel, out_shape, scratch=(), flops=0, moved=0):
    return pl.pallas_call(
        kernel,
        out_shape=out_shape,
        scratch_shapes=scratch,
        compiler_params=pltpu.CompilerParams(vmem_limit_bytes=VMEM_LIMIT),
        cost_estimate=pl.CostEstimate(flops=flops, bytes_accessed=moved, transcendentals=0),
    )


class Grid:
    names = ("zh", "zl", "y", "x", "c")

    def __init__(self, mesh):
        experts, heads = mesh.shape["expert"], mesh.shape["head"]
        self.shape = (2, experts // 4, 2, heads // 2, 2)
        self.experts, self.heads = experts, heads
        self.total = experts * heads

    def size(self, name):
        return self.shape[self.names.index(name)]

    def coords(self, linear):
        out = []
        for extent in reversed(self.shape):
            out.append(linear % extent)
            linear = linear // extent
        return dict(zip(self.names, reversed(out)))

    def linear(self, coords):
        at = 0
        for name, extent in zip(self.names, self.shape):
            at = at * extent + coords[name] % extent
        return at

    def me(self, name):
        linear = lax.axis_index("expert") * self.heads + lax.axis_index("head")
        return self.coords(linear)[name]

    def send(self, value, target):
        pairs = [(i, self.linear(target(self.coords(i)))) for i in range(self.total)]
        return lax.ppermute(value, ("expert", "head"), pairs)

    def shift(self, value, name, by):
        return self.send(value, lambda at: {**at, name: at[name] - by})

    def gather(self, value, name):
        extent, own = self.size(name), self.me(name)
        parts = [value] + [self.shift(value, name, by) for by in range(1, extent)]
        if extent == 2:
            return jnp.where(own == 0, jnp.stack(parts), jnp.stack(parts[::-1]))
        return jnp.roll(jnp.stack(parts), own, axis=0)

    def scatter_sum(self, value, name):
        extent, own = self.size(name), self.me(name)
        if extent == 2:
            kept = jnp.where(own == 0, value[0], value[1])
            others = [self.shift(jnp.where(own == 0, value[1], value[0]), name, 1)]
        else:
            value = jnp.roll(value, -own, axis=0)
            kept = value[0]
            others = [self.shift(value[by], name, -by) for by in range(1, extent)]
        total = kept.astype(single)
        for other in others:
            total = total + other.astype(single)
        return total.astype(value.dtype)


def gelu_tanh(values):
    return jax.nn.gelu(values, approximate=True)


def per_device(
    grid,
    tokens,
    segment_ids,
    task_ids,
    task_table,
    weight_qkv,
    weight_out,
    gain_one,
    gain_two,
    weight_router,
    weight_in,
    weight_hidden,
    cotangent,
):
    expert_count, head_count = grid.experts, grid.heads
    head_index = lax.axis_index("head")
    row_count, model_width = tokens.shape
    cap = 4 * row_count // expert_count
    deep, wide = weight_qkv.shape[1:]
    padded = -(-expert_count // 16) * 16

    pieces = jnp.concatenate([weight_qkv, weight_out.T[None]]).astype(bfloat)
    small = jnp.concatenate(
        [gain_one[None], gain_two[None], weight_router.T]
    ).astype(bfloat).reshape(-1)
    small_rows = -(-small.shape[0] // wide)
    small = jnp.pad(small, (0, small_rows * wide - small.shape[0])).reshape(small_rows, wide)
    packed = jnp.concatenate([pieces.reshape(4 * deep, wide), small])
    for name in ("zh", "zl", "y", "x", "c"):
        packed = grid.gather(packed, name)
    packed = packed.transpose(4, 3, 2, 1, 0, 5, 6).reshape(
        expert_count, head_count, 4 * deep + small_rows, wide
    )
    weights = (
        packed[:, :, : 4 * deep]
        .reshape(expert_count, head_count, 4, deep, wide)
        .transpose(2, 0, 3, 1, 4)
        .reshape(4, model_width, model_width)
    )
    smalls = packed[:, 0, 4 * deep :].reshape(expert_count, -1)[:, : (2 + expert_count) * deep]
    smalls = smalls.reshape(expert_count, 2 + expert_count, deep).transpose(1, 0, 2)
    smalls = smalls.reshape(2 + expert_count, model_width)
    gain1, gain2 = smalls[0:1].astype(single), smalls[1:2].astype(single)
    router = jnp.pad(smalls[2:], ((0, padded - expert_count), (0, 0)))
    wqkv, wot = weights[:3], weights[3]

    own_segments = lax.dynamic_slice_in_dim(segment_ids, head_index * row_count, row_count)
    chosen = task_table[task_ids[own_segments]]
    expert_range = jnp.arange(expert_count, dtype=jnp.int32)
    flat_choice = chosen.reshape(-1)
    expert_marks = (flat_choice[:, None] == expert_range).astype(jnp.int32)
    running = jnp.cumsum(expert_marks, axis=0)
    slot_index = jnp.sum((running - 1) * expert_marks, axis=1)
    destination = jnp.where(slot_index < cap, flat_choice * cap + slot_index, expert_count * cap)
    first, second = chosen[:, 0][None], chosen[:, 1][None]
    segc = own_segments[:, None]
    starts = [min(max(at - SPAN, 0), row_count - WINDOW) for at in range(0, row_count, BLOCK)]
    segw = jnp.stack([own_segments[at : at + WINDOW] for at in starts])

    shape = jax.ShapeDtypeStruct
    proj, attn, res, two_low, stat, gate = whole_call(
        forward_kernel,
        (
            shape((3, row_count, model_width), bfloat),
            shape((row_count, model_width), bfloat),
            shape((row_count, model_width), single),
            shape((row_count, model_width), bfloat),
            shape((row_count, LANES), single),
            shape((padded, row_count), single),
        ),
        flops=2 * 5 * row_count * model_width**2,
        moved=16 * row_count * model_width,
    )(tokens, wqkv, wot, gain1, gain2, router, segc, segw, first, second)

    expert_in = lax.all_gather(weight_in.astype(bfloat), "head", axis=1, tiled=True)[0]
    expert_hidden = lax.all_gather(weight_hidden.astype(bfloat), "head", axis=1, tiled=True)[0]
    pair_marks = chosen[:, :, None] == expert_range
    gate_weights = jnp.sum(jnp.where(pair_marks, gate[:expert_count].T[:, None, :], 0.0), axis=-1)
    send_rows = (
        jnp.zeros((expert_count * cap + 1, model_width), bfloat)
        .at[destination]
        .set(jnp.repeat(two_low, 2, axis=0))
    )
    send_rows = send_rows[:-1].reshape(expert_count, cap, model_width)
    received = lax.all_to_all(send_rows, "expert", split_axis=0, concat_axis=0, tiled=True)
    flat_in = received.reshape(-1, model_width)
    hidden_pre = jnp.dot(flat_in, expert_in, preferred_element_type=single)
    activated, gelu_pullback = jax.vjp(gelu_tanh, hidden_pre)
    act_low = activated.astype(bfloat)
    results = jnp.dot(act_low, expert_hidden, preferred_element_type=single).astype(bfloat)
    returned = lax.all_to_all(
        results.reshape(expert_count, cap, model_width),
        "expert",
        split_axis=0,
        concat_axis=0,
        tiled=True,
    )
    zero_row = jnp.zeros((1, model_width), bfloat)
    back_pairs = (
        jnp.concatenate([returned.reshape(-1, model_width), zero_row])[destination]
        .astype(single)
        .reshape(row_count, 2, model_width)
    )
    output = (res + jnp.sum(gate_weights[:, :, None] * back_pairs, axis=1)).astype(bfloat)
    grad_top = cotangent.astype(single)
    grad_pairs = (
        (gate_weights[:, :, None] * grad_top[:, None, :]).reshape(-1, model_width).astype(bfloat)
    )
    send_grad = (
        jnp.zeros((expert_count * cap + 1, model_width), bfloat).at[destination].set(grad_pairs)
    )
    send_grad = send_grad[:-1].reshape(expert_count, cap, model_width)
    grad_gates = jnp.sum(back_pairs * grad_top[:, None, :], axis=-1)
    inner = jnp.sum(jnp.where(pair_marks, grad_gates[:, :, None], 0.0), axis=1)
    inner = jnp.pad(inner, ((0, 0), (0, padded - expert_count))).T
    grad_results = lax.all_to_all(send_grad, "expert", split_axis=0, concat_axis=0, tiled=True)
    flat_grad = grad_results.reshape(-1, model_width)
    grad_act = jnp.einsum("rd,fd->rf", flat_grad, expert_hidden, preferred_element_type=single)
    grad_hidden_local = jnp.einsum("rf,rd->fd", act_low, flat_grad, preferred_element_type=single)
    grad_pre = gelu_pullback(grad_act)[0].astype(bfloat)
    grad_in_local = jnp.einsum("rd,rf->df", flat_in, grad_pre, preferred_element_type=single)
    grad_rows = jnp.einsum("rf,df->rd", grad_pre, expert_in, preferred_element_type=single).astype(
        bfloat
    )
    grad_back = lax.all_to_all(
        grad_rows.reshape(expert_count, cap, model_width),
        "expert",
        split_axis=0,
        concat_axis=0,
        tiled=True,
    )
    grad_copies = jnp.concatenate([grad_back.reshape(-1, model_width), zero_row])[
        destination
    ].astype(single)
    grad_copies = jnp.sum(grad_copies.reshape(row_count, 2, model_width), axis=1)

    grad_tokens, grad_w, grad_gain1, grad_gain2, grad_router = whole_call(
        backward_kernel,
        (
            shape((row_count, model_width), single),
            shape((4, model_width, model_width), bfloat),
            shape((1, model_width), single),
            shape((1, model_width), single),
            shape((padded, model_width), single),
        ),
        scratch=[
            pltpu.VMEM((row_count, model_width), single),
            pltpu.VMEM((row_count, model_width), bfloat),
            pltpu.VMEM((row_count, model_width), bfloat),
            pltpu.VMEM((3, row_count, model_width), bfloat),
            pltpu.VMEM((row_count, model_width), single),
            pltpu.VMEM((row_count, model_width), single),
            pltpu.VMEM((row_count, model_width), bfloat),
        ],
        flops=2 * 10 * row_count * model_width**2,
        moved=24 * row_count * model_width,
    )(
        tokens, cotangent, res, two_low, proj, attn, stat, wqkv, wot, gain1, gain2, router,
        segc, segw, gate, inner, grad_copies,
    )

    pieces = (
        grad_w.reshape(4, expert_count, deep, head_count, wide)
        .transpose(1, 3, 0, 2, 4)
        .reshape(expert_count, head_count, 4 * deep, wide)
    )
    smalls = jnp.concatenate([grad_gain1, grad_gain2, grad_router[:expert_count]]).astype(bfloat)
    smalls = smalls.reshape(2 + expert_count, expert_count, deep).transpose(1, 0, 2)
    smalls = smalls.reshape(expert_count, -1)
    smalls = jnp.pad(smalls, ((0, 0), (0, small_rows * wide - smalls.shape[1])))
    smalls = jnp.broadcast_to(
        smalls.reshape(expert_count, 1, small_rows, wide),
        (expert_count, head_count, small_rows, wide),
    )
    packed = jnp.concatenate([pieces, smalls], axis=2)
    packed = packed.reshape(*grid.shape, 4 * deep + small_rows, wide).transpose(4, 3, 2, 1, 0, 5, 6)
    for name in ("c", "x", "y", "zl", "zh"):
        packed = grid.scatter_sum(packed, name)
    pieces = packed[: 4 * deep].reshape(4, deep, wide).astype(single)
    smalls = packed[4 * deep :].reshape(-1)[: (2 + expert_count) * deep].astype(single)
    smalls = smalls.reshape(2 + expert_count, deep)
    expert_totals = (
        lax.psum_scatter(
            grad_in_local[None].astype(jnp.bfloat16), "head", scatter_dimension=1, tiled=True
        ).astype(jnp.float32),
        lax.psum_scatter(
            grad_hidden_local[None].astype(jnp.bfloat16), "head", scatter_dimension=1, tiled=True
        ).astype(jnp.float32),
    )
    return (
        output,
        grad_tokens,
        pieces[:3],
        pieces[3].T,
        smalls[0],
        smalls[1],
        smalls[2:].T,
        expert_totals[0],
        expert_totals[1],
    )


def solution(mesh):
    grid = Grid(mesh)
    placed = (
        P(("expert", "head"), None),
        P("expert"),
        P(),
        P(),
        P(None, "expert", "head"),
        P("head", "expert"),
        P("expert"),
        P("expert"),
        P("expert", None),
        P("expert", "head", None),
        P("expert", "head", None),
        P(("expert", "head"), None),
    )

    def step(*arrays):
        return per_device(grid, *arrays)

    return jax.shard_map(
        step,
        mesh=mesh,
        in_specs=placed,
        out_specs=(
            P(("expert", "head"), None),
            P(("expert", "head"), None),
            P(None, "expert", "head"),
            P("head", "expert"),
            P("expert"),
            P("expert"),
            P("expert", None),
            P("expert", "head", None),
            P("expert", "head", None),
        ),
        check_vma=False,
    )
```

time: 1130 us -> 676 us (0.60)
  blocking collectives: 221 us -> 0 us
  waiting for transfers between devices: 425 us -> 293 us
  matrix products: 208 us -> 114 us
  Pallas kernels: 0 us -> 48.3 us
  other arithmetic: 97.1 us -> 53.1 us
  local copies, waits for them, and re-layouts: 139 us -> 110 us
  starting transfers between devices: 20.4 us -> 33.1 us
    all_gather x3 -> x0, blocking collectives: 171 us -> none  [the longest x1 109 us: per_device(): lax.all_gather(weight_router.astype(bfloat), 'expert', axis=0, tiled=True)]
    reduce_scatter x3 -> x0, waiting for transfers between devices: 165 us -> none  [the longest x1 62.8 us: per_device(): lax.psum_scatter(grad_out_local.astype(jnp.bfloat16), 'expert', scatter_d...]
    unnamed x13 -> x4, waiting for transfers between devices: 102 us -> 0.07 us
    dot_general x37 -> x0, matrix products: 93.7 us -> none  [the longest x4 15.6 us: attend_back(): jnp.einsum('qhd,khd->hqk', grad_attended, values_block, preferred_element...]
    all_to_all x1, waiting for transfers between devices: 0.01 us -> 66.2 us  [per_device(): lax.all_to_all(send_rows, 'expert', split_axis=0, concat_axis=0, tiled=True)]
    pallas_call x0 -> x2, Pallas kernels: none -> 48.3 us  [the longest x1 28.6 us: per_device(): whole_call(backward_kernel, (shape((row_count, model_width), single), sha...]
    unnamed x2 -> x0, blocking collectives: 44.5 us -> none
    ppermute x0 -> x10, waiting for transfers between devices: none -> 38 us  [send(): return lax.ppermute(value, ('expert', 'head'), pairs)]
  transfers between devices with their start and end apart: 15 -> 18, of which waited for: 10 -> 14; matrix products, arithmetic and copies ran while one was open for 26% -> 28% of each run, Pallas kernels for 0% -> 4%
where the time goes in v1:
time: 676 us; the launch traced here: 666 us
  waiting for transfers between devices  293 us (43%)
  matrix products  114 us (17%)
  local copies, waits for them, and re-layouts  110 us (16%)
  other arithmetic  53.1 us (8%)
  Pallas kernels  48.3 us (7%)
  starting transfers between devices  33.1 us (5%)
  between operations  15 us (2%)
    all_to_all x1, waiting for transfers between devices, per_device(): lax.all_to_all(grad_rows.reshape(expert_count, cap, model_width), 'expert...  78.7 us
    all_to_all x1, waiting for transfers between devices, per_device(): lax.all_to_all(send_rows, 'expert', split_axis=0, concat_axis=0, tiled=True)  66.2 us
    all_to_all x1, waiting for transfers between devices, per_device(): lax.all_to_all(results.reshape(expert_count, cap, model_width), 'expert',...  42.3 us
    all_to_all x1, waiting for transfers between devices, per_device(): lax.all_to_all(send_grad, 'expert', split_axis=0, concat_axis=0, tiled=True)  42.3 us
    ppermute x10, waiting for transfers between devices, send(): return lax.ppermute(value, ('expert', 'head'), pairs)  38 us
    dot_general x1, matrix products, per_device(): jnp.einsum('rd,fd->rf', flat_grad, expert_hidden, preferred_element_type=...  32.1 us
    pallas_call x1, Pallas kernels, per_device(): whole_call(backward_kernel, (shape((row_count, model_width), single), sha...  28.6 us
    all_gather x1, waiting for transfers between devices, per_device(): lax.all_gather(weight_in.astype(bfloat), 'head', axis=1, tiled=True)[0]  25 us
  transfers between devices with their start and end apart: 18, of which 14 were waited for; matrix products, arithmetic and copies ran while one was open for 28% of the time, Pallas kernels for 4%

profile of v1, /device:TPU:0, one launch (start us, length us, event | category | flops | bytes accessed | tf_op | source)
XLA Modules:
  0.0 665.9 jit_solution(17135662272972386547)
XLA Ops:
  10.4 4.1 collective-permute-start
  15.2 4.5 gather_fusion
  19.9 2.8 gather_fusion.1
  24.7 2.3 reduce-window.6
  30.3 4.7 collective-permute-done.2
  37.4 9.7 %collective-permute-done.3 = bf16[2,2,2,261,128]{4,2,3,1,0:T(2,128)(2,1)S(1)} collective-permute-done((bf16[2,2,2,261,128]{4,2,3,1,0:T(2,128)(2,1)S(1)}, bf16[2,2,2,261,128]{4,2,3,1,0:T(2,128)(2,1)S(1)}, u32[]{:S(2)}, u32[]{:S(2)}) %collective-permute-start.3) | collective-permute-done | bytes 534560 | tf_op jit(solution)/shard_map/ppermute | solution.py:239
  54.6 2.6 copy.150
  57.1 3.6 slice.155.wqkv
  64.1 19.7 %shard_map.187 = (bf16[3,1024,512]{2,1,0:T(8,128)(2,1)}, bf16[1024,512]{1,0:T(8,128)(2,1)}, f32[1024,512]{1,0:T(8,128)}, bf16[1024,512]{1,0:T(8,128)(2,1)}, f32[1024,128]{1,0:T(8,128)}, /*index=5*/f32[16,1024]{1,0:T(8,128)}) custom-call(bf16[1024,512]{1,0:T(8,128)(2,1)} %tok.3, bf16[3,512,512]{2,1,0:T(8,128)(2,1)} %slice.155.wqkv, ...), custom_call_target="tpu_custom_call" | custom-call | flops 2684354560 | bytes 8388608 | tf_op jit(solution)/shard_map/pallas_call | solution.py:331
  83.8 2.3 broadcast_in_dim.79
  86.1 2.2 reshape.731
  88.3 12.7 %scatter_custom_fusion = bf16[4097,512]{1,0:T(8,128)(2,1)} fusion(s32[2048]{0:T(1024)S(1)} %bitcast.216, bf16[2048,512]{1,0:T(8,128)(2,1)} %reshape.731, bf16[]{:T(256)} %constant.140.clone.1), kind=kCustom, calls=%fused_computation.32 | custom fusion | bytes 4195840 | tf_op jit(solution)/shard_map/scatter | solution.py:352
  101.0 4.4 slice.215
  105.5 4.7 all-to-all-start
  110.3 3.0 mul.122
  113.4 6.1 mul.126
  120.0 13.6 %scatter_custom_fusion.1 = bf16[4097,512]{1,0:T(8,128)(2,1)} fusion(s32[2048]{0:T(1024)S(1)} %bitcast.217, bf16[]{:T(256)} %constant.140.clone.1, f32[2048,512]{1,0:T(8,128)} %mul.126, f32[2048]{0:T(1024)S(1)} %mul.124), kind=kCustom, calls=%fused_computation.30 | custom fusion | flops 2097152 | bytes 8397826 | tf_op jit(solution)/shard_map/scatter | solution.py:380
  133.6 4.5 slice.216
  138.1 66.2 %all-to-all-done = bf16[8,512,512]{2,1,0:T(8,128)(2,1)} async-done(((bf16[8,512,512]{2,1,0:T(8,128)(2,1)}), bf16[8,512,512]{2,1,0:T(8,128)(2,1)}, u32[]{:S(2)}, u32[]{:S(2)}) %all-to-all-start) | async-done | bytes 4194336 | tf_op jit(solution)/shard_map/all_to_all | solution.py:355
  204.3 4.7 all-to-all-start.2
  210.9 25.0 %all-gather.3.cloned.1.call-done = bf16[1,512,2048]{2,1,0:T(8,128)(2,1)} async-done(((bf16[1,128,2048]{2,1,0:T(8,128)(2,1)}), bf16[1,512,2048]{2,1,0:T(8,128)(2,1)}) %all-gather.3.cloned.1.call-update) | async-done | bytes 2097168 | tf_op jit(solution)/shard_map/all_gather | solution.py:345
  235.9 23.9 %multiply_convert_fusion = (bf16[4096,2048]{1,0:T(8,128)(2,1)}, f32[4096,2048]{1,0:T(8,128)}) fusion(bf16[4096,512]{1,0:T(8,128)(2,1)} %bitcast.42, bf16[1,512,2048]{2,1,0:T(8,128)(2,1)} %all-gather.3.cloned.1.call-done), kind=kOutput, calls=%fused_computation.15 | convolution fusion | flops 8665432064 | bytes 56623104 | tf_op jit(solution)/shard_map/dot_general | solution.py:357
  260.0 42.3 %all-to-all-done.2 = bf16[8,512,512]{2,1,0:T(8,128)(2,1)} async-done(((bf16[8,512,512]{2,1,0:T(8,128)(2,1)}), bf16[8,512,512]{2,1,0:T(8,128)(2,1)}, u32[]{:S(2)}, u32[]{:S(2)}) %all-to-all-start.2) | async-done | bytes 4194336 | tf_op jit(solution)/shard_map/all_to_all | solution.py:386
  302.3 32.1 %fusion.6 = bf16[4096,2048]{1,0:T(8,128)(2,1)} fusion(f32[4096,2048]{1,0:T(8,128)} %get-tuple-element.55, bf16[4096,512]{1,0:T(8,128)(2,1)} %bitcast.49, bf16[1,2048,512]{2,1,0:T(8,128)(2,1)} %all-gather.5.cloned.1.call-done), kind=kOutput, calls=%fused_computation.14 | convolution fusion | flops 8757706752 | bytes 56623104 | tf_op jit(solution)/shard_map/rd,fd->rf/dot_general | solution.py:388
  334.4 14.3 %convolution_convert_fusion = bf16[4096,512]{1,0:T(8,128)(2,1)} fusion(bf16[4096,2048]{1,0:T(8,128)(2,1)} %fusion.6, bf16[1,512,2048]{2,1,0:T(8,128)(2,1)S(1)} %copy-done.17), kind=kOutput, calls=%fused_computation.16 | convolution fusion | flops 8592031744 | bytes 23068672 | tf_op jit(solution)/shard_map/rf,df->rd/dot_general | solution.py:392
  348.6 4.7 all-to-all-start.3
  353.4 13.8 %convolution_convert_fusion.1 = bf16[4096,512]{1,0:T(8,128)(2,1)} fusion(bf16[4096,2048]{1,0:T(8,128)(2,1)} %get-tuple-element.54, bf16[1,2048,512]{2,1,0:T(8,128)(2,1)S(1)} %copy-done.18), kind=kOutput, calls=%fused_computation.17 | convolution fusion | flops 8592031744 | bytes 23068672 | tf_op jit(solution)/shard_map/dot_general | solution.py:360
  367.2 78.7 %all-to-all-done.3 = bf16[8,512,512]{2,1,0:T(8,128)(2,1)} async-done(((bf16[8,512,512]{2,1,0:T(8,128)(2,1)}), bf16[8,512,512]{2,1,0:T(8,128)(2,1)}, u32[]{:S(2)}, u32[]{:S(2)}) %all-to-all-start.3) | async-done | bytes 4194336 | tf_op jit(solution)/shard_map/all_to_all | solution.py:395
  445.9 4.6 all-to-all-start.1
  450.5 14.7 %fusion.7 = bf16[1,512,2048]{2,1,0:T(8,128)(2,1)} fusion(bf16[4096,512]{1,0:T(8,128)(2,1)} %bitcast.42, bf16[4096,2048]{1,0:T(8,128)(2,1)} %fusion.6), kind=kOutput, calls=%fused_computation.23 | convolution fusion | flops 8590983168 | bytes 23068672 | tf_op jit(solution)/shard_map/rd,rf->df/dot_general | solution.py:391
  466.9 14.8 %fusion.8 = bf16[1,2048,512]{2,1,0:T(8,128)(2,1)} fusion(bf16[4096,2048]{1,0:T(8,128)(2,1)} %get-tuple-element.54, bf16[4096,512]{1,0:T(8,128)(2,1)} %bitcast.49), kind=kOutput, calls=%fused_computation.24 | convolution fusion | flops 8590983168 | bytes 23068672 | tf_op jit(solution)/shard_map/rf,rd->fd/dot_general | solution.py:389
  481.7 4.6 concatenate.148
  486.3 10.3 %gather_fusion.3 = bf16[2048,512]{1,0:T(8,128)(2,1)S(1)} fusion(bf16[4097,512]{1,0:T(8,128)(2,1)} %concatenate.148, s32[2048]{0:T(1024)S(1)} %broadcast_clamp_fusion), kind=kCustom, calls=%fused_computation.3 | custom fusion | bytes 4202496 | tf_op jit(solution)/shard_map/gather | solution.py:402
  496.6 4.0 reshape.687
  500.6 42.3 %all-to-all-done.1 = bf16[8,512,512]{2,1,0:T(8,128)(2,1)} async-done(((bf16[8,512,512]{2,1,0:T(8,128)(2,1)}), bf16[8,512,512]{2,1,0:T(8,128)(2,1)}, u32[]{:S(2)}, u32[]{:S(2)}) %all-to-all-start.1) | async-done | bytes 4194336 | tf_op jit(solution)/shard_map/all_to_all | solution.py:361
  543.0 4.4 concatenate.147
  547.4 10.3 %gather_fusion.2 = bf16[2048,512]{1,0:T(8,128)(2,1)S(1)} fusion(bf16[4097,512]{1,0:T(8,128)(2,1)} %concatenate.147, s32[2048]{0:T(1024)S(1)} %broadcast_clamp_fusion), kind=kCustom, calls=%fused_computation.2 | custom fusion | bytes 4202496 | tf_op jit(solution)/shard_map/gather | solution.py:370
  557.7 4.0 reshape.686
  561.7 11.5 %multiply_reduce_fusion = (f32[1024,2]{1,0:T(8,128)S(1)}, f32[1024,512]{1,0:T(8,128)}) fusion(f32[1024,2,512]{2,1,0:T(2,128)} %reshape.686, f32[1024,512]{1,0:T(8,128)} %convert_element_type.180, f32[1024,2]{1,0:T(8,128)S(1)} %copy-done.4), kind=kLoop, calls=%fused_computation.19 | loop fusion | flops 3667968 | bytes 8404992 | tf_op jit(solution)/shard_map/reduce_sum | solution.py:383
  574.0 8.5 %reduce_sum.62.copies = f32[1024,512]{1,0:T(8,128)} reduce(f32[1024,2,512]{2,1,0:T(2,128)} %reshape.687, f32[]{:T(128)} %constant.144.clone.1), dimensions={1}, to_apply=%region_9.10 | reduce | flops 524288 | bytes 6291460 | tf_op jit(solution)/shard_map/reduce_sum | solution.py:405
  582.5 28.6 %shard_map.188 = (f32[1024,512]{1,0:T(8,128)}, bf16[4,512,512]{2,1,0:T(8,128)(2,1)}, f32[1,512]{1,0:T(1,128)}, f32[1,512]{1,0:T(1,128)}, f32[16,512]{1,0:T(8,128)}) custom-call(bf16[1024,512]{1,0:T(8,128)(2,1)} %tok.3, bf16[1024,512]{1,0:T(8,128)(2,1)} %cot.1, f32[1024,512]{1,0:T(8,128)} %get-tuple-element.20.res, bf16[1024,512]{1,0:T(8,128)(2,1)} %get-tuple-element.22.two, ...), custom_call_target="tpu_custom_call" | custom-call | flops 5368709120 | bytes 12582912 | tf_op jit(solution)/shard_map/pallas_call | solution.py:407
  611.1 3.9 reshape.683
  619.9 2.7 collective-permute-done.5
  625.0 12.7 %collective-permute-done.6 = bf16[2,2,2,261,128]{4,2,3,1,0:T(2,128)(2,1)S(1)} collective-permute-done((bf16[2,2,2,261,128]{4,2,3,1,0:T(2,128)(2,1)S(1)}, bf16[2,2,2,261,128]{4,2,3,1,0:T(2,128)(2,1)S(1)}, u32[]{:S(2)}, u32[]{:S(2)}) %collective-permute-start.6) | collective-permute-done | bytes 534560 | tf_op jit(solution)/shard_map/ppermute | solution.py:239
  639.5 6.2 collective-permute-done.7
  648.1 2.1 convert_element_type.214
  651.0 2.2 collective-permute-start.9
  653.2 3.0 add_convert_fusion
  (163 shorter events, 42.3 us)
Async XLA Ops:
  7.2 8.0 %copy-start = (s32[1024]{0:T(1024)S(1)}, s32[1024]{0:T(1024)}, u32[]{:S(2)}) copy-start(s32[1024]{0:T(1024)} %param.14) | copy-start | bytes 12292
  7.2 12.6 %copy-start.16 = (s32[64,2]{0,1:T(2,128)S(1)}, s32[64,2]{0,1:T(2,128)}, u32[]{:S(2)}) copy-start(s32[64,2]{0,1:T(2,128)} %param.15) | copy-start | bytes 1540
  10.4 12.6 %collective-permute-start = (bf16[261,128]{1,0:T(8,128)(2,1)S(1)}, bf16[261,128]{1,0:T(8,128)(2,1)S(1)}, u32[]{:S(2)}, u32[]{:S(2)}) collective-permute-start(bf16[261,128]{1,0:T(8,128)(2,1)S(1)} %get-tuple-element.43), channel_id=1, source_target_pairs={{0,16},{1,17},{2,18},{3,19},{4,20},{5,21},{6,22},{7,23},{8,24},{9,... | collective-permute-start | bytes 200456 | tf_op jit(solution)/shard_map/ppermute | solution.py:239
  23.1 5.1 collective-permute-start.1
  28.2 6.8 %collective-permute-start.2 = (bf16[2,2,261,128]{3,2,1,0:T(8,128)(2,1)S(1)}, bf16[2,2,261,128]{3,2,1,0:T(8,128)(2,1)S(1)}, u32[]{:S(2)}, u32[]{:S(2)}) collective-permute-start(bf16[2,2,261,128]{3,2,1,0:T(8,128)(2,1)S(1)} %maximum_select_fusion.6), channel_id=1, source_target_pairs={{0,4},{1,5},{2,6},{3,7},{4,0},{5,1},{6,2},{7,3},{8,12},{9,13},{10,... | collective-permute-start | bytes 801800 | tf_op jit(solution)/shard_map/ppermute | solution.py:239
  35.5 11.6 %collective-permute-start.3 = (bf16[2,2,2,261,128]{4,2,3,1,0:T(2,128)(2,1)S(1)}, bf16[2,2,2,261,128]{4,2,3,1,0:T(2,128)(2,1)S(1)}, u32[]{:S(2)}, u32[]{:S(2)}) collective-permute-start(bf16[2,2,2,261,128]{4,2,3,1,0:T(2,128)(2,1)S(1)} %copy.144), channel_id=1, source_target_pairs={{0,2},{1,3},{2,0},{3,1},{4,6},{5,7},{6,4},{7,5},{8,10},{9,11},{10,... | collective-permute-start | bytes 1603592 | tf_op jit(solution)/shard_map/ppermute | solution.py:239
  48.2 3.8 collective-permute-start.4
  51.8 68.3 %copy-start.11 = (s32[2048,1]{0,1:T(1,128)}, s32[2048,1]{0,1:T(1,128)S(1)}, u32[]{:S(2)}) copy-start(s32[2048,1]{0,1:T(1,128)S(1)} %compare_select_fusion) | copy-start | bytes 24580
  105.5 4.9 copy-start.5
  105.5 98.8 %all-to-all-start = ((bf16[8,512,512]{2,1,0:T(8,128)(2,1)}), bf16[8,512,512]{2,1,0:T(8,128)(2,1)}, u32[]{:S(2)}, u32[]{:S(2)}) async-start(bf16[8,512,512]{2,1,0:T(8,128)(2,1)} %bitcast.187), calls=%async_computation | async-start | bytes 8388608 | tf_op jit(solution)/shard_map/all_to_all | solution.py:355
  110.3 9.1 %copy-start.9 = (s32[1024,2]{0,1:T(2,128)}, s32[1024,2]{0,1:T(2,128)S(1)}, u32[]{:S(2)}) copy-start(s32[1024,2]{0,1:T(2,128)S(1)} %copy.155) | copy-start | bytes 24580
  113.4 6.1 copy-start.13
  119.8 13.8 %copy-start.3 = (f32[1024,2]{1,0:T(8,128)}, f32[1024,2]{1,0:T(8,128)S(1)}, u32[]{:S(2)}) copy-start(f32[1024,2]{1,0:T(8,128)S(1)} %copy.156) | copy-start | bytes 24580
  204.3 4.7 copy-start.7
  204.3 5.7 copy-start.8
  204.3 98.0 %all-to-all-start.2 = ((bf16[8,512,512]{2,1,0:T(8,128)(2,1)}), bf16[8,512,512]{2,1,0:T(8,128)(2,1)}, u32[]{:S(2)}, u32[]{:S(2)}) async-start(bf16[8,512,512]{2,1,0:T(8,128)(2,1)} %bitcast.186), calls=%async_computation.2 | async-start | bytes 8388608 | tf_op jit(solution)/shard_map/all_to_all | solution.py:386
  209.0 26.9 %all-gather.3.cloned.1.call-start = ((), (), s32[]{:S(2)}) async-start(), calls=%async_computation.6 | async-start | bytes 2621440 | tf_op jit(solution)/shard_map/all_gather | solution.py:345
  209.9 50.1 %all-gather.5.cloned.1.call-start = ((), (), s32[]{:S(2)}) async-start(), calls=%async_computation.7 | async-start | bytes 2621440 | tf_op jit(solution)/shard_map/all_gather | solution.py:346
  302.3 32.1 %copy-start.17 = (bf16[1,512,2048]{2,1,0:T(8,128)(2,1)S(1)}, bf16[1,512,2048]{2,1,0:T(8,128)(2,1)}, u32[]{:S(2)}) copy-start(bf16[1,512,2048]{2,1,0:T(8,128)(2,1)} %all-gather.3.cloned.1.call-done) | copy-start | bytes 6291460
  348.6 4.7 copy-start.18
  348.6 97.2 %all-to-all-start.3 = ((bf16[8,512,512]{2,1,0:T(8,128)(2,1)}), bf16[8,512,512]{2,1,0:T(8,128)(2,1)}, u32[]{:S(2)}, u32[]{:S(2)}) async-start(bf16[8,512,512]{2,1,0:T(8,128)(2,1)} %bitcast.197), calls=%async_computation.3 | async-start | bytes 8388608 | tf_op jit(solution)/shard_map/all_to_all | solution.py:395
  445.9 97.1 %all-to-all-start.1 = ((bf16[8,512,512]{2,1,0:T(8,128)(2,1)}), bf16[8,512,512]{2,1,0:T(8,128)(2,1)}, u32[]{:S(2)}, u32[]{:S(2)}) async-start(bf16[8,512,512]{2,1,0:T(8,128)(2,1)} %bitcast.196), calls=%async_computation.1 | async-start | bytes 8388608 | tf_op jit(solution)/shard_map/all_to_all | solution.py:361
  450.4 14.8 %copy-start.6 = (bf16[1024,512]{1,0:T(8,128)(2,1)S(1)}, bf16[1024,512]{1,0:T(8,128)(2,1)}, u32[]{:S(2)}) copy-start(bf16[1024,512]{1,0:T(8,128)(2,1)} %cot.1) | copy-start | bytes 3145732
  450.5 195.5 %reduce-scatter.3.cloned.1.call-start = ((), (), s32[]{:S(2)}) async-start(), calls=%async_computation.8 | async-start | bytes 2621440 | tf_op jit(solution)/shard_map/reduce_scatter | solution.py:453
  465.2 1.7 copy-start.12
  465.2 182.9 %reduce-scatter.5.cloned.1.call-start = ((), (), s32[]{:S(2)}) async-start(), calls=%async_computation.9 | async-start | bytes 2621440 | tf_op jit(solution)/shard_map/reduce_scatter | solution.py:456
  557.7 4.0 copy-start.4
  561.7 11.6 %copy-start.10 = (s32[1024,2]{0,1:T(2,128)S(1)}, s32[1024,2]{0,1:T(2,128)}, u32[]{:S(2)}) copy-start(s32[1024,2]{0,1:T(2,128)} %copy-done.9) | copy-start | bytes 24580
  611.1 6.9 %copy-start.15 = (f32[1,512]{1,0:T(1,128)S(1)}, f32[1,512]{1,0:T(1,128)}, u32[]{:S(2)}) copy-start(f32[1,512]{1,0:T(1,128)} %get-tuple-element.28) | copy-start | bytes 6148
  611.1 7.1 %copy-start.14 = (f32[1,512]{1,0:T(1,128)S(1)}, f32[1,512]{1,0:T(1,128)}, u32[]{:S(2)}) copy-start(f32[1,512]{1,0:T(1,128)} %get-tuple-element.29) | copy-start | bytes 6148
  619.8 2.8 collective-permute-start.5
  623.4 29.8 %copy-start.2 = (f32[1024,512]{1,0:T(8,128)S(1)}, f32[1024,512]{1,0:T(8,128)}, u32[]{:S(2)}) copy-start(f32[1024,512]{1,0:T(8,128)} %get-tuple-element.32) | copy-start | bytes 6291460
  623.5 14.2 %collective-permute-start.6 = (bf16[2,2,2,261,128]{4,2,3,1,0:T(2,128)(2,1)S(1)}, bf16[2,2,2,261,128]{4,2,3,1,0:T(2,128)(2,1)S(1)}, u32[]{:S(2)}, u32[]{:S(2)}) collective-permute-start(bf16[2,2,2,261,128]{4,2,3,1,0:T(2,128)(2,1)S(1)} %copy.166), channel_id=1, source_target_pairs={{0,2},{1,3},{2,0},{3,1},{4,6},{5,7},{6,4},{7,5},{8,10},{9,11},{10,... | collective-permute-start | bytes 1603592 | tf_op jit(solution)/shard_map/ppermute | solution.py:239
  638.0 7.8 %collective-permute-start.7 = (bf16[2,2,261,128]{3,2,0,1:T(8,128)(2,1)S(1)}, bf16[2,2,261,128]{3,2,0,1:T(8,128)(2,1)S(1)}, u32[]{:S(2)}, u32[]{:S(2)}) collective-permute-start(bf16[2,2,261,128]{3,2,0,1:T(8,128)(2,1)S(1)} %fusion.23), channel_id=1, source_target_pairs={{0,4},{1,5},{2,6},{3,7},{4,0},{5,1},{6,2},{7,3},{8,12},{9,13},{10,... | collective-permute-start | bytes 801800 | tf_op jit(solution)/shard_map/ppermute | solution.py:239
  645.9 5.1 collective-permute-start.8
  646.0 12.9 %copy-start.1 = (s32[1024]{0:T(1024)S(1)}, s32[1024]{0:T(1024)}, u32[]{:S(2)}) copy-start(s32[1024]{0:T(1024)} %param.14) | copy-start | bytes 12292
  651.0 5.3 collective-permute-start.9
Sparse Core Ops, SparseCore 0:
  211.9 23.8 all-gather.2
  237.4 22.5 all-gather.4
  465.3 32.6 reduce-scatter.2
  500.6 31.4 reduce-scatter.4

commit v2 on v1

--- a/solution.py
+++ b/solution.py
@@ -12,6 +12,10 @@
 WINDOW = BLOCK + 2 * SPAN
 CHUNK = 256
 LANES = 128
+TILE = 256
+HALF = 128
+EXTRA = 16
+ABSENT = -1e6
 
 EPSILON = 1e-05
 NEGATIVE = -1e30
@@ -59,11 +63,37 @@
     return pl.multiple_of(jnp.clip(block * BLOCK - SPAN, 0, rows - WINDOW), SPAN)
 
 
+def fetch_weights(heads, core, own, other, weights, sem):
+    wide = weights.shape[2] // heads
+    copies = []
+    if own.shape == weights.shape:
+        copies = [pltpu.make_async_copy(own, weights, sem.at[0, 0])]
+        heads = 0
+    for by in range(heads // 2):
+        for i, (ref, at) in enumerate(((own, core), (other, 1 - core))):
+            start = (2 * by + at) * wide
+            start = pl.multiple_of(start, LANES)
+            copies.append(
+                pltpu.make_async_copy(
+                    ref.at[:, :, pl.ds(by * wide, wide)],
+                    weights.at[:, :, pl.ds(start, wide)],
+                    sem.at[i, by],
+                )
+            )
+    for copy in copies:
+        copy.start()
+    for copy in copies:
+        copy.wait()
+
+
 def forward_kernel(
-    tok, wqkv, wot, gain1, gain2, router, segc, segw, first, second,
-    proj, attn, res, two, stat, gate,
+    cap, heads, meta, tok, weights_own, weights_other, gain1, gain2, router, segc, segw, first, second, slots,
+    proj, attn, res, two, stat, gate, *refs,
 ):
+    *parcels, weights, sem = refs
     rows, width = tok.shape
+    fetch_weights(heads, meta[4 * len(parcels)], weights_own, weights_other, weights, sem)
+    wqkv, wot = weights, weights.at[3]
 
     def project(step, carry):
         at = pl.ds(pl.multiple_of(step * CHUNK, CHUNK), CHUNK)
@@ -115,19 +145,144 @@
         return carry
 
     lax.fori_loop(0, rows // BLOCK, attend, 0)
+    pack_parcels(cap, meta, two, slots, parcels)
+
+
+def pack_parcels(cap, meta, rows, slots, parcels):
+    tile = min(TILE, cap)
+    for at, parcel in enumerate(parcels):
+        for local in range(2):
+            for step in range(cap // tile):
+
+                @pl.when(meta[2 * len(parcels) + 2 * at + local] > step * tile)
+                def _():
+                    ones = onehot(slots[pl.ds(meta[2 * at + local], 1), :], step * tile, tile)
+                    parcel[local * cap + step * tile : local * cap + (step + 1) * tile, :] = dot_nn(
+                        ones, rows[...]
+                    ).astype(bfloat)
+
+
+def split_two(values):
+    high = values.astype(bfloat)
+    return high, (values - high.astype(single)).astype(bfloat)
+
+
+def pack_rows(rows):
+    at = lax.broadcasted_iota(jnp.int32, (EXTRA, rows.shape[1]), 0)
+    out = jnp.zeros((EXTRA, rows.shape[1]), single)
+    for local in range(2):
+        high = rows[local : local + 1, :].astype(bfloat).astype(single)
+        out = jnp.where(at == 2 * local, high, out)
+        out = jnp.where(at == 2 * local + 1, rows[local : local + 1, :] - high, out)
+    return out.astype(bfloat)
+
+
+def unpack_row(packed, local):
+    packed = packed.astype(single)
+    return packed[2 * local : 2 * local + 1, :] + packed[2 * local + 1 : 2 * local + 2, :]
+
+
+def routing_kernel(
+    cap, segments, tasks, table, weight_in, weight_hidden,
+    first, second, slots, other, kept, piece,
+):
+    rows = segments.shape[1]
+    deep, hidden = weight_in.shape[1:]
+    width = piece.shape[1]
+    for part in range(hidden // width):
+        piece[part * deep : (part + 1) * deep, :] = weight_in[
+            0, :, part * width : (part + 1) * width
+        ].astype(bfloat)
+    piece[hidden // width * deep :, :] = weight_hidden[0].astype(bfloat)
+    names = lax.broadcasted_iota(jnp.int32, (table.shape[1], tasks.shape[1]), 0)
+    experts = dot_nn(table[...], jnp.where(names == tasks[...], 1.0, 0.0).astype(bfloat))
+    experts = experts.astype(bfloat)
+    chosen = jnp.zeros((table.shape[0], rows), single)
+    for start in range(0, tasks.shape[1], 1024):
+        size = min(1024, tasks.shape[1] - start)
+        at = lax.broadcasted_iota(jnp.int32, (size, rows), 0) + start
+        ones = jnp.where(at == segments[...], 1.0, 0.0).astype(bfloat)
+        chosen = chosen + dot_nn(experts[:, start : start + size], ones)
+    zero, one = chosen[0:1, :], chosen[1:2, :]
+    first[...] = zero.astype(jnp.int32)
+    second[...] = one.astype(jnp.int32)
+    which = lax.broadcasted_iota(jnp.int32, slots.shape, 0).astype(single)
+    is_first, is_second = which == zero, which == one
+    other[...] = jnp.where(is_first, one, jnp.where(is_second, zero, 0.0))
+    marks = jnp.where(is_first | is_second, 1.0, 0.0)
+    earlier = lax.broadcasted_iota(jnp.int32, (rows, rows), 0) < lax.broadcasted_iota(
+        jnp.int32, (rows, rows), 1
+    )
+    places = dot_nn(marks.astype(bfloat), jnp.where(earlier, 1.0, 0.0).astype(bfloat))
+    inside = (marks > 0.5) & (places < cap)
+    slots[...] = jnp.where(inside, places, ABSENT)
+    total = jnp.sum(jnp.where(inside, 1.0, 0.0), axis=1, keepdims=True)
+    kept[...] = jnp.broadcast_to(total, kept.shape).astype(jnp.int32)
+
+
+def cotangent_kernel(cap, meta, cot, slots, other, waited, *parcels):
+    pack_parcels(cap, meta, cot, slots, parcels)
+    tile = min(TILE, cap)
+    at_row = lax.broadcasted_iota(jnp.int32, (EXTRA, tile), 0)
+    which = lax.broadcasted_iota(jnp.int32, (other.shape[0], 1), 0)
+    others = other[...].astype(bfloat)
+    for at, parcel in enumerate(parcels):
+        for step in range(cap // tile):
+            out = jnp.zeros((EXTRA, tile), single)
+            for local in range(2):
+                chosen = meta[2 * at + local]
+                number = meta[2 * len(parcels) + 2 * at + local]
+                ones = onehot(slots[pl.ds(chosen, 1), :], step * tile, tile)
+                moved = dot_nt(others, ones)
+                moved = jnp.sum(jnp.where(which == chosen, moved, 0.0), axis=0, keepdims=True)
+                high = number // 16 * 16
+                out = jnp.where(at_row == local, moved, out)
+                out = jnp.where(at_row == 2 + 2 * local, high.astype(single), out)
+                out = jnp.where(at_row == 3 + 2 * local, (number - high).astype(single), out)
+            parcel[2 * cap :, step * tile : (step + 1) * tile] = out.astype(bfloat)
+
+
+def output_kernel(providers, cap, meta, res, slots, *refs):
+    parcels, out = refs[:providers], refs[providers]
+    for step in range(res.shape[0] // CHUNK):
+        at = slice(step * CHUNK, (step + 1) * CHUNK)
+        out[at, :] = (res[at, :] + returned_rows(parcels, cap, meta, slots, at)).astype(bfloat)
+
+
+def returned_rows(parcels, cap, meta, slots, at):
+    total = 0.0
+    for provider, parcel in enumerate(parcels):
+        for local in range(2):
+            ones = onehot(slots[pl.ds(meta[2 * provider + local], 1), at], 0, cap)
+            total = total + dot_tn(ones, parcel[local * cap : (local + 1) * cap, :])
+    return total
 
 
 def backward_kernel(
-    tok, cot, res, two, proj, attn, stat, wqkv, wot, gain1, gain2, router, segc, segw,
-    gate, inner, copies,
-    grad_tok, grad_w, grad_gain1, grad_gain2, grad_router,
-    grad_res, grad_attn, grad_heads, grad_proj, grad_key, grad_value, normed,
+    providers, cap, heads, waited, meta,
+    tok, cot, res, two, proj, attn, stat, weights_own, weights_other, gain1, gain2, router, segc, segw, gate, slots,
+    *refs,
 ):
+    parcels = refs[:providers]
+    (
+        grad_tok, grad_w, grad_gain1, grad_gain2, grad_router,
+        products, grad_res, grad_attn, grad_heads, grad_proj, grad_key, grad_value, normed,
+        weights, sem,
+    ) = refs[providers + waited :]
     rows, width = tok.shape
-    weights = gate[...]
-    inner_products = inner[...]
-    grad_logits = weights * (
-        inner_products - jnp.sum(weights * inner_products, axis=0, keepdims=True)
+    fetch_weights(heads, meta[4 * providers], weights_own, weights_other, weights, sem)
+    wqkv, wot = weights, weights.at[3]
+    products[...] = jnp.zeros_like(products)
+    for provider in range(providers):
+        for local in range(2):
+            chosen = meta[2 * provider + local]
+            ones = onehot(slots[pl.ds(chosen, 1), :], 0, cap)
+            moved = dot_nn(parcels[provider][2 * cap :, :cap], ones)
+            products[pl.ds(chosen, 1), :] = unpack_row(moved, local)
+    gates = gate[...]
+    inner_products = products[...]
+    grad_logits = gates * (
+        inner_products - jnp.sum(gates * inner_products, axis=0, keepdims=True)
     )
     logits_high = grad_logits.astype(bfloat)
     logits_low = (grad_logits - logits_high.astype(single)).astype(bfloat)
@@ -143,7 +298,8 @@
     for step in range(rows // CHUNK):
         at = slice(step * CHUNK, (step + 1) * CHUNK)
         scaled, inverse = normalise(res[at, :])
-        grad_normed = copies[at, :].astype(single) + dot_tn(grad_logits[:, at], router_twice)
+        grad_normed = dot_tn(grad_logits[:, at], router_twice)
+        grad_normed = grad_normed + returned_rows(parcels, cap, meta, slots, at)
         grad_gain2[...] += jnp.sum(grad_normed * scaled, axis=0, keepdims=True)
         grad_row = cot[at, :].astype(single) + norm_pull(grad_normed, scaled, inverse, gain2[...])
         grad_res[at, :] = grad_row
@@ -195,13 +351,275 @@
         grad_w[part] = dot_tn(normed[...], grad_proj[part]).astype(bfloat)
 
 
-def whole_call(kernel, out_shape, scratch=(), flops=0, moved=0):
+def onehot(slots, base, rows):
+    places = lax.broadcasted_iota(jnp.int32, (rows, slots.shape[1]), 0).astype(single)
+    return jnp.where(places == slots - base, 1.0, 0.0).astype(bfloat)
+
+
+def gelu_both(values):
+    square = values * values
+    rate = 0.7978845608028654 + 0.035677408136300125 * square
+    slope = 0.7978845608028654 + 0.10703222440890037 * square
+    bent = jnp.tanh(values * rate)
+    half = 0.5 + 0.5 * bent
+    return values * half, half + values * (0.5 - 0.5 * (bent * bent)) * slope
+
+
+def expert_kernel(sources, heads, first, meta, router, *refs):
+    refs = list(refs)
+
+    def take(count):
+        taken = refs[:count]
+        del refs[:count]
+        return taken
+
+    rows_in, grads_in = take(sources), take(sources)
+    pieces = take(2 * heads)
+    if not first:
+        take(4)
+    saved = take(4)
+    outs, grads = take(sources), take(sources)
+    (
+        win, wout, row_buf, grad_buf, out_buf, copy_buf, product_buf, top,
+        st_x, st_g, st_act, st_pre, table, w_sem, in_sem, s_sem, out_sem,
+    ) = refs
+    width = row_buf.shape[2]
+    cap = row_buf.shape[1] // 2
+    hidden = wout.shape[1]
+    deep, wide = width // heads, hidden // heads
+    head_x, head_c = meta[0], meta[1]
+    staged = (st_x, st_g, st_act, st_pre)
+
+    def weight_copies(local):
+        at = 0
+        for by_x in range(heads // 2):
+            for by_c in range(2):
+                head = lax.rem(head_x + by_x, heads // 2) * 2 + lax.rem(head_c + by_c, 2)
+                piece = pieces[(local * (heads // 2) + by_x) * 2 + by_c]
+                for part in range(hidden // width):
+                    yield pltpu.make_async_copy(
+                        piece.at[pl.ds(part * deep, deep), :],
+                        win.at[
+                            local,
+                            pl.ds(pl.multiple_of(head * deep, deep), deep),
+                            pl.ds(part * width, width),
+                        ],
+                        w_sem.at[local, at],
+                    )
+                    at += 1
+                yield pltpu.make_async_copy(
+                    piece.at[pl.ds(hidden // width * deep, wide), :],
+                    wout.at[local, pl.ds(pl.multiple_of(head * wide, wide), wide), :],
+                    w_sem.at[local, at],
+                )
+                at += 1
+
+    def source_copies():
+        for source in range(sources):
+            yield pltpu.make_async_copy(rows_in[source], row_buf.at[source], in_sem.at[0, source])
+            yield pltpu.make_async_copy(grads_in[source], grad_buf.at[source], in_sem.at[1, source])
+
+    for copy in weight_copies(0):
+        copy.start()
+    for copy in source_copies():
+        copy.start()
+    for copy in weight_copies(1):
+        copy.start()
+    out_buf[...] = jnp.zeros_like(out_buf)
+    copy_buf[...] = jnp.zeros_like(copy_buf)
+    product_buf[...] = jnp.zeros_like(product_buf)
+
+    def save_copies(slot, local, tile):
+        at = pl.ds(pl.multiple_of(tile * TILE, TILE), TILE)
+        return [
+            pltpu.make_async_copy(stage.at[slot], save.at[local, at, :], s_sem.at[slot, i])
+            for i, (stage, save) in enumerate(zip(staged, saved))
+        ]
+
+    halves = []
+    for local in range(2):
+        number = 0
+        for source in range(sources):
+            for half in range(cap // HALF):
+                table[local, number] = source * (cap // HALF) + half
+                filled = meta[6 + local * sources + source] > half * HALF
+                number = number + jnp.where(filled, 1, 0)
+        halves.append(number)
+    eye = lax.broadcasted_iota(jnp.int32, (HALF, HALF), 0) == lax.broadcasted_iota(
+        jnp.int32, (HALF, HALF), 1
+    )
+    column = lax.broadcasted_iota(jnp.int32, (HALF, LANES), 1).astype(single)
+    for copy in source_copies():
+        copy.wait()
+    done = 0
+    for local in range(2):
+        for copy in weight_copies(local):
+            copy.wait()
+        number = halves[local]
+
+        def place(tile, half):
+            entry = table[local, 2 * tile + half]
+            step = lax.rem(entry, cap // HALF)
+            start = pl.multiple_of(step * HALF, HALF)
+            rows = pl.ds(pl.multiple_of(local * cap + start, HALF), HALF)
+            return entry // (cap // HALF), rows, pl.ds(start, HALF)
+
+        def one_tile(tile, done):
+            slot = lax.rem(done, 2)
+
+            @pl.when(done >= 2)
+            def _():
+                for copy in save_copies(slot, local, tile):
+                    copy.wait()
+
+            for half in range(2):
+                at = pl.ds(half * HALF, HALF)
+
+                @pl.when(2 * tile + half < number)
+                def _():
+                    source, rows, lanes = place(tile, half)
+                    st_x[slot, at, :] = row_buf[source, rows, :]
+                    other = grad_buf[source, pl.ds(2 * cap, EXTRA), lanes].astype(single)
+                    other = jnp.where(eye, other[local : local + 1, :], 0.0)
+                    other = jnp.sum(other, axis=1, keepdims=True)
+                    logits = dot_nt(row_buf[source, rows, :], router[...])
+                    own = meta[2 + local].astype(single)
+                    own = jnp.sum(jnp.where(column == own, logits, 0.0), axis=1, keepdims=True)
+                    other = jnp.sum(jnp.where(column == other, logits, 0.0), axis=1, keepdims=True)
+                    peak = jnp.maximum(own, other)
+                    own, other = jnp.exp(own - peak), jnp.exp(other - peak)
+                    gate = own / (own + other)
+                    grad = grad_buf[source, rows, :]
+                    top[at, :width] = grad.astype(single)
+                    top[at, width:] = jnp.broadcast_to(gate, (HALF, LANES))
+                    st_g[slot, at, :] = (gate * grad.astype(single)).astype(bfloat)
+
+                @pl.when(2 * tile + half >= number)
+                def _():
+                    st_x[slot, at, :] = jnp.zeros((HALF, width), bfloat)
+                    st_g[slot, at, :] = jnp.zeros((HALF, width), bfloat)
+                    top[at, :] = jnp.zeros((HALF, width + LANES), single)
+
+            rows_low, grad_low = st_x[slot], st_g[slot]
+            for part in range(hidden // width):
+                cols = slice(part * width, (part + 1) * width)
+                pre = dot_nn(rows_low, win[local, :, cols])
+                grad_act = dot_nt(grad_low, wout[local, cols, :])
+                act, slope = gelu_both(pre)
+                st_act[slot, :, cols] = act.astype(bfloat)
+                st_pre[slot, :, cols] = (slope * grad_act).astype(bfloat)
+            result = dot_nn(st_act[slot], wout[local]).astype(bfloat).astype(single)
+            grad_copy = dot_nt(st_pre[slot], win[local]).astype(bfloat)
+            product = jnp.sum(top[:, :width] * result, axis=1, keepdims=True)
+            weighted = (top[:, width : width + 1] * result).astype(bfloat)
+            for half in range(2):
+                at = slice(half * HALF, (half + 1) * HALF)
+
+                @pl.when(2 * tile + half < number)
+                def _():
+                    source, rows, lanes = place(tile, half)
+                    out_buf[source, rows, :] = weighted[at]
+                    copy_buf[source, rows, :] = grad_copy[at]
+                    product_buf[source, local : local + 1, lanes] = jnp.sum(
+                        jnp.where(eye, product[at], 0.0), axis=0, keepdims=True
+                    )
+
+            for copy in save_copies(slot, local, meta[4 + local] + tile):
+                copy.start()
+            return done + 1
+
+        done = lax.fori_loop(0, (number + 1) // 2, one_tile, done)
+
+    def result_copies():
+        for source in range(sources):
+            yield pltpu.make_async_copy(copy_buf.at[source], grads[source], out_sem.at[0, source])
+            yield pltpu.make_async_copy(out_buf.at[source], outs[source], out_sem.at[1, source])
+
+    for source in range(sources):
+        copy_buf[source, 2 * cap :, :cap] = pack_rows(product_buf[source])
+    for copy in result_copies():
+        copy.start()
+    for back in (1, 2):
+
+        @pl.when(done >= back)
+        def _():
+            for copy in save_copies(lax.rem(done - back, 2), 0, 0):
+                copy.wait()
+
+    for copy in result_copies():
+        copy.wait()
+
+
+def weight_kernel(heads, meta, save_x, save_g, save_act, save_pre, *refs):
+    outs = refs[: 2 * heads]
+    grad_in, grad_out, buf_x, buf_g, buf_act, buf_pre, sem = refs[2 * heads :]
+    width, hidden = grad_in.shape
+    deep, wide = width // heads, hidden // heads
+    buffers = (buf_x, buf_g, buf_act, buf_pre)
+
+    def fetch(slot, local, tile):
+        at = pl.ds(pl.multiple_of(tile * TILE, TILE), TILE)
+        return [
+            pltpu.make_async_copy(save.at[local, at, :], buf.at[slot], sem.at[slot, i])
+            for i, (save, buf) in enumerate(zip((save_x, save_g, save_act, save_pre), buffers))
+        ]
+
+    for local in (1, 0):
+        tiles = meta[2 + local]
+        grad_in[...] = jnp.zeros_like(grad_in)
+        grad_out[...] = jnp.zeros_like(grad_out)
+
+        @pl.when(tiles > 0)
+        def _():
+            for copy in fetch(0, local, 0):
+                copy.start()
+
+        def one_tile(tile, carry):
+            slot = lax.rem(tile, 2)
+
+            @pl.when(tile + 1 < tiles)
+            def _():
+                for copy in fetch(1 - slot, local, tile + 1):
+                    copy.start()
+
+            for copy in fetch(slot, local, tile):
+                copy.wait()
+            for part in range(hidden // width):
+                cols = slice(part * width, (part + 1) * width)
+                grad_in[:, cols] += dot_tn(buf_x[slot], buf_pre[slot, :, cols])
+                grad_out[:, cols] += dot_tn(buf_g[slot], buf_act[slot, :, cols])
+            return carry
+
+        lax.fori_loop(0, tiles, one_tile, 0)
+        for by_x in range(heads // 2):
+            for by_c in range(2):
+                head = lax.rem(meta[0] + by_x, heads // 2) * 2 + lax.rem(meta[1] + by_c, 2)
+                out = outs[(local * (heads // 2) + by_x) * 2 + by_c]
+                for part in range(hidden // width):
+                    out[part * deep : (part + 1) * deep, :] = grad_in[
+                        pl.ds(pl.multiple_of(head * deep, deep), deep),
+                        part * width : (part + 1) * width,
+                    ].astype(bfloat)
+                block = grad_out[:, pl.ds(pl.multiple_of(head * wide, wide), wide)]
+                out[hidden // width * deep :, :] = block.T.astype(bfloat)
+
+
+def whole_call(kernel, out_shape, scratch=(), micros=1, in_specs=None, out_specs=None, aliases=None):
+    specs = {}
+    if in_specs is not None:
+        specs["in_specs"] = in_specs
+    if out_specs is not None:
+        specs["out_specs"] = out_specs
     return pl.pallas_call(
         kernel,
         out_shape=out_shape,
         scratch_shapes=scratch,
+        input_output_aliases=aliases or {},
         compiler_params=pltpu.CompilerParams(vmem_limit_bytes=VMEM_LIMIT),
-        cost_estimate=pl.CostEstimate(flops=flops, bytes_accessed=moved, transcendentals=0),
+        cost_estimate=pl.CostEstimate(
+            flops=micros * 1153000000, bytes_accessed=0, transcendentals=0
+        ),
+        **specs,
     )
 
 
@@ -238,8 +656,11 @@
         pairs = [(i, self.linear(target(self.coords(i)))) for i in range(self.total)]
         return lax.ppermute(value, ("expert", "head"), pairs)
 
+    def move(self, value, **by):
+        return self.send(value, lambda at: {name: at[name] - by.get(name, 0) for name in at})
+
     def shift(self, value, name, by):
-        return self.send(value, lambda at: {**at, name: at[name] - by})
+        return self.move(value, **{name: by})
 
     def gather(self, value, name):
         extent, own = self.size(name), self.me(name)
@@ -263,8 +684,8 @@
         return total.astype(value.dtype)
 
 
-def gelu_tanh(values):
-    return jax.nn.gelu(values, approximate=True)
+def after(value, *others):
+    return lax.optimization_barrier((value, *others))[0]
 
 
 def per_device(
@@ -296,116 +717,217 @@
     small_rows = -(-small.shape[0] // wide)
     small = jnp.pad(small, (0, small_rows * wide - small.shape[0])).reshape(small_rows, wide)
     packed = jnp.concatenate([pieces.reshape(4 * deep, wide), small])
-    for name in ("zh", "zl", "y", "x", "c"):
-        packed = grid.gather(packed, name)
-    packed = packed.transpose(4, 3, 2, 1, 0, 5, 6).reshape(
-        expert_count, head_count, 4 * deep + small_rows, wide
-    )
-    weights = (
-        packed[:, :, : 4 * deep]
-        .reshape(expert_count, head_count, 4, deep, wide)
-        .transpose(2, 0, 3, 1, 4)
-        .reshape(4, model_width, model_width)
-    )
-    smalls = packed[:, 0, 4 * deep :].reshape(expert_count, -1)[:, : (2 + expert_count) * deep]
-    smalls = smalls.reshape(expert_count, 2 + expert_count, deep).transpose(1, 0, 2)
-    smalls = smalls.reshape(2 + expert_count, model_width)
+    packed = grid.gather(grid.gather(packed, "zh"), "zl")
+    barely = packed
+    packed = grid.gather(packed, "y")
+    partly = packed
+    smalls = packed.transpose(2, 1, 0, 3, 4).reshape(expert_count, -1)[:, 4 * deep * wide :]
+    smalls = smalls[:, : (2 + expert_count) * deep].reshape(expert_count, 2 + expert_count, deep)
+    smalls = smalls.transpose(1, 0, 2).reshape(2 + expert_count, model_width)
     gain1, gain2 = smalls[0:1].astype(single), smalls[1:2].astype(single)
     router = jnp.pad(smalls[2:], ((0, padded - expert_count), (0, 0)))
-    wqkv, wot = weights[:3], weights[3]
+    packed = grid.gather(packed[..., : 4 * deep, :], "x")
+    packed = packed.transpose(0, 3, 2, 1, 4, 5).reshape(-1, expert_count, 4, deep, wide)
+    packed = packed.transpose(2, 1, 3, 0, 4).reshape(4, model_width, -1)
+    if wide % LANES:
+        packed = grid.gather(packed, "c").reshape(2, 4, model_width, -1, wide)
+        packed = packed.transpose(1, 2, 3, 0, 4).reshape(4, model_width, model_width)
+        weights = (packed, packed)
+    else:
+        weights = (packed, grid.shift(packed, "c", 1))
 
     own_segments = lax.dynamic_slice_in_dim(segment_ids, head_index * row_count, row_count)
-    chosen = task_table[task_ids[own_segments]]
-    expert_range = jnp.arange(expert_count, dtype=jnp.int32)
-    flat_choice = chosen.reshape(-1)
-    expert_marks = (flat_choice[:, None] == expert_range).astype(jnp.int32)
-    running = jnp.cumsum(expert_marks, axis=0)
-    slot_index = jnp.sum((running - 1) * expert_marks, axis=1)
-    destination = jnp.where(slot_index < cap, flat_choice * cap + slot_index, expert_count * cap)
-    first, second = chosen[:, 0][None], chosen[:, 1][None]
+    shape = jax.ShapeDtypeStruct
+    vmem, hbm = pl.BlockSpec(memory_space=pltpu.VMEM), pl.BlockSpec(memory_space=pl.ANY)
+    smem = pl.BlockSpec(memory_space=pltpu.SMEM)
+    table = jnp.pad(task_table.T, ((0, 16 - task_table.shape[1]), (0, 0))).astype(bfloat)
+    hidden = weight_in.shape[2]
+    deep_in = weight_in.shape[1]
+    piece = shape((hidden // model_width * deep_in + weight_hidden.shape[1], model_width), bfloat)
+    first, second, slots, other, kept, own_piece = whole_call(
+        lambda *refs: routing_kernel(cap, *refs),
+        [shape((1, row_count), jnp.int32)] * 2
+        + [shape((padded, row_count), single)] * 2
+        + [shape((padded, LANES), jnp.int32), piece],
+        micros=3,
+    )(own_segments[None], task_ids[None], table, weight_in, weight_hidden)
+    kept = kept[:, 0]
     segc = own_segments[:, None]
     starts = [min(max(at - SPAN, 0), row_count - WINDOW) for at in range(0, row_count, BLOCK)]
     segw = jnp.stack([own_segments[at : at + WINDOW] for at in starts])
 
-    shape = jax.ShapeDtypeStruct
-    proj, attn, res, two_low, stat, gate = whole_call(
-        forward_kernel,
-        (
+    names = {name: grid.me(name) for name in grid.names}
+    extent = grid.size("zl")
+    offsets = [(dl, dy) for dl in range(extent) for dy in range(2)]
+    offsets.sort(key=lambda by: by[0] * by[1] != 0)
+    providers = len(offsets)
+
+    def expert_of(zl, y, local):
+        return ((names["zh"] + local) % 2 * extent + zl % extent) * 2 + y % 2
+
+    def meta_of(experts):
+        experts = jnp.stack(experts).astype(jnp.int32)
+        return jnp.concatenate([experts, kept[experts], names["c"][None]])
+
+    targets = meta_of(
+        [expert_of(names["zl"] - dl, names["y"] - dy, k) for dl, dy in offsets for k in range(2)]
+    )
+    row_parcel = shape((2 * cap, model_width), bfloat)
+    parcel = shape((2 * cap + EXTRA, model_width), bfloat)
+    cot_parcels = whole_call(
+        lambda *refs: cotangent_kernel(cap, *refs),
+        [parcel] * providers,
+        in_specs=[smem] + [vmem] * 3 + [hbm],
+        micros=10,
+    )(targets, cotangent, slots, other, partly)
+    proj, attn, res, two_low, stat, gate, *row_parcels = whole_call(
+        lambda *refs: forward_kernel(cap, head_count, *refs),
+        [
             shape((3, row_count, model_width), bfloat),
             shape((row_count, model_width), bfloat),
             shape((row_count, model_width), single),
             shape((row_count, model_width), bfloat),
             shape((row_count, LANES), single),
             shape((padded, row_count), single),
-        ),
-        flops=2 * 5 * row_count * model_width**2,
-        moved=16 * row_count * model_width,
-    )(tokens, wqkv, wot, gain1, gain2, router, segc, segw, first, second)
-
-    expert_in = lax.all_gather(weight_in.astype(bfloat), "head", axis=1, tiled=True)[0]
-    expert_hidden = lax.all_gather(weight_hidden.astype(bfloat), "head", axis=1, tiled=True)[0]
-    pair_marks = chosen[:, :, None] == expert_range
-    gate_weights = jnp.sum(jnp.where(pair_marks, gate[:expert_count].T[:, None, :], 0.0), axis=-1)
-    send_rows = (
-        jnp.zeros((expert_count * cap + 1, model_width), bfloat)
-        .at[destination]
-        .set(jnp.repeat(two_low, 2, axis=0))
-    )
-    send_rows = send_rows[:-1].reshape(expert_count, cap, model_width)
-    received = lax.all_to_all(send_rows, "expert", split_axis=0, concat_axis=0, tiled=True)
-    flat_in = received.reshape(-1, model_width)
-    hidden_pre = jnp.dot(flat_in, expert_in, preferred_element_type=single)
-    activated, gelu_pullback = jax.vjp(gelu_tanh, hidden_pre)
-    act_low = activated.astype(bfloat)
-    results = jnp.dot(act_low, expert_hidden, preferred_element_type=single).astype(bfloat)
-    returned = lax.all_to_all(
-        results.reshape(expert_count, cap, model_width),
-        "expert",
-        split_axis=0,
-        concat_axis=0,
-        tiled=True,
-    )
-    zero_row = jnp.zeros((1, model_width), bfloat)
-    back_pairs = (
-        jnp.concatenate([returned.reshape(-1, model_width), zero_row])[destination]
-        .astype(single)
-        .reshape(row_count, 2, model_width)
-    )
-    output = (res + jnp.sum(gate_weights[:, :, None] * back_pairs, axis=1)).astype(bfloat)
-    grad_top = cotangent.astype(single)
-    grad_pairs = (
-        (gate_weights[:, :, None] * grad_top[:, None, :]).reshape(-1, model_width).astype(bfloat)
-    )
-    send_grad = (
-        jnp.zeros((expert_count * cap + 1, model_width), bfloat).at[destination].set(grad_pairs)
-    )
-    send_grad = send_grad[:-1].reshape(expert_count, cap, model_width)
-    grad_gates = jnp.sum(back_pairs * grad_top[:, None, :], axis=-1)
-    inner = jnp.sum(jnp.where(pair_marks, grad_gates[:, :, None], 0.0), axis=1)
-    inner = jnp.pad(inner, ((0, 0), (0, padded - expert_count))).T
-    grad_results = lax.all_to_all(send_grad, "expert", split_axis=0, concat_axis=0, tiled=True)
-    flat_grad = grad_results.reshape(-1, model_width)
-    grad_act = jnp.einsum("rd,fd->rf", flat_grad, expert_hidden, preferred_element_type=single)
-    grad_hidden_local = jnp.einsum("rf,rd->fd", act_low, flat_grad, preferred_element_type=single)
-    grad_pre = gelu_pullback(grad_act)[0].astype(bfloat)
-    grad_in_local = jnp.einsum("rd,rf->df", flat_in, grad_pre, preferred_element_type=single)
-    grad_rows = jnp.einsum("rf,df->rd", grad_pre, expert_in, preferred_element_type=single).astype(
-        bfloat
-    )
-    grad_back = lax.all_to_all(
-        grad_rows.reshape(expert_count, cap, model_width),
-        "expert",
-        split_axis=0,
-        concat_axis=0,
-        tiled=True,
-    )
-    grad_copies = jnp.concatenate([grad_back.reshape(-1, model_width), zero_row])[
-        destination
-    ].astype(single)
-    grad_copies = jnp.sum(grad_copies.reshape(row_count, 2, model_width), axis=1)
+        ]
+        + [row_parcel] * providers,
+        in_specs=[smem, vmem, hbm, hbm] + [vmem] * 8,
+        scratch=[
+            pltpu.VMEM((4, model_width, model_width), bfloat),
+            pltpu.SemaphoreType.DMA((2, head_count // 2)),
+        ],
+        micros=28,
+    )(targets, tokens, *weights, gain1, gain2, router, segc, segw, first, second, slots)
+
+    pieces = {(0, 0, 0): after(own_piece, cot_parcels[0])}
+    pieces[1, 0, 0] = after(grid.shift(after(own_piece, barely), "zh", 1), two_low)
+    for by_x in range(1, head_count // 2):
+        for local in range(2):
+            pieces[local, by_x, 0] = grid.shift(pieces[local, 0, 0], "x", by_x)
+    sources = []
+    for (dl, dy), *both in zip(offsets, row_parcels, cot_parcels):
+        if dl or dy:
+            both = [grid.move(value, zl=dl, y=dy) for value in both]
+            both[1] = after(both[1], two_low)
+        numbers = both[1][2 * cap + 2 : 2 * cap + 6, 0].astype(jnp.int32)
+        sources.append((*both, numbers[0::2] + numbers[1::2]))
+    for by_x in range(1, head_count // 2):
+        pieces[1, by_x, 0] = after(pieces[1, by_x, 0], sources[-1][0])
+    for by_x in range(head_count // 2):
+        for local in range(2):
+            pieces[local, by_x, 1] = grid.shift(pieces[local, by_x, 0], "c", 1)
+    piece_keys = [(k, bx, bc) for k in range(2) for bx in range(head_count // 2) for bc in range(2)]
+    piece_list = [pieces[key] for key in piece_keys]
+
+    order = [0] + list(range(providers - 1, 0, -1))
+    groups = [order[at : at + 2] for at in range(0, providers, 2)]
+    save_tiles = sum(-(-len(group) * cap // TILE) for group in groups)
+    save_shapes = [
+        shape((2, save_tiles * TILE, cols), bfloat)
+        for cols in (model_width, model_width, hidden, hidden)
+    ]
+    own_experts = jnp.stack([expert_of(names["zl"], names["y"], local) for local in range(2)])
+    wide_router = jnp.pad(router, ((0, LANES - padded), (0, 0)))
+    saved = []
+    tiles_before = jnp.zeros((2,), jnp.int32)
+    results = {}
+    for group in groups:
+        count = len(group)
+        numbers = jnp.stack([sources[s][2] for s in group], axis=1)
+        meta = jnp.concatenate(
+            [names["x"][None], names["c"][None], own_experts, tiles_before, numbers.reshape(-1)]
+        ).astype(jnp.int32)
+        half_tiles = jnp.sum((numbers + HALF - 1) // HALF, axis=1)
+        tiles_before = tiles_before + (half_tiles + 1) // 2
+        inputs = [meta, wide_router] + [sources[s][part] for part in range(2) for s in group]
+        inputs += piece_list + saved
+        before = 2 + 2 * count + len(piece_list)
+        outs = whole_call(
+            lambda *refs, count=count, new=not saved: expert_kernel(count, head_count, new, *refs),
+            save_shapes + [parcel] * (2 * count),
+            in_specs=[smem, vmem] + [hbm] * (2 * count + len(piece_list) + len(saved)),
+            out_specs=[hbm] * (4 + 2 * count),
+            aliases={before + i: i for i in range(len(saved))},
+            scratch=[
+                pltpu.VMEM((2, model_width, hidden), bfloat),
+                pltpu.VMEM((2, hidden, model_width), bfloat),
+                pltpu.VMEM((count, *row_parcel.shape), bfloat),
+                pltpu.VMEM((count, *parcel.shape), bfloat),
+                pltpu.VMEM((count, *parcel.shape), bfloat),
+                pltpu.VMEM((count, *parcel.shape), bfloat),
+                pltpu.VMEM((count, 8, cap), single),
+                pltpu.VMEM((TILE, model_width + LANES), single),
+                pltpu.VMEM((2, TILE, model_width), bfloat),
+                pltpu.VMEM((2, TILE, model_width), bfloat),
+                pltpu.VMEM((2, TILE, hidden), bfloat),
+                pltpu.VMEM((2, TILE, hidden), bfloat),
+                pltpu.SMEM((2, count * cap // HALF + 1), jnp.int32),
+                pltpu.SemaphoreType.DMA((2, head_count * (hidden // model_width + 1))),
+                pltpu.SemaphoreType.DMA((2, count)),
+                pltpu.SemaphoreType.DMA((2, 4)),
+                pltpu.SemaphoreType.DMA((2, count)),
+            ],
+            micros=25,
+        )(*inputs)
+        saved = list(outs[:4])
+        for i, s in enumerate(group):
+            results[s] = [outs[4 + i], outs[4 + count + i]]
+    out_parcels, grad_parcels = [], []
+    for s, (dl, dy) in enumerate(offsets):
+        out_part, grad_part = results[s]
+        if dl or dy:
+            grad_part, out_part = (grid.move(v, zl=-dl, y=-dy) for v in (grad_part, out_part))
+        out_parcels.append(out_part)
+        grad_parcels.append(grad_part)
+    weight_meta = jnp.concatenate([names["x"][None], names["c"][None], tiles_before])
+    done = whole_call(
+        lambda *refs: weight_kernel(head_count, *refs),
+        [piece] * len(piece_keys),
+        in_specs=[smem] + [hbm] * 4,
+        scratch=[
+            pltpu.VMEM((model_width, hidden), single),
+            pltpu.VMEM((model_width, hidden), single),
+            pltpu.VMEM((2, TILE, model_width), bfloat),
+            pltpu.VMEM((2, TILE, model_width), bfloat),
+            pltpu.VMEM((2, TILE, hidden), bfloat),
+            pltpu.VMEM((2, TILE, hidden), bfloat),
+            pltpu.SemaphoreType.DMA((2, 4)),
+        ],
+        micros=24,
+    )(weight_meta.astype(jnp.int32), *saved)
+    done = lax.optimization_barrier((*done, *grad_parcels[1:]))
+    grad_parcels = grad_parcels[:1] + list(done[len(piece_keys) :])
+    grads = dict(zip(piece_keys, done))
+
+    def add(kept, other):
+        return (kept.astype(single) + other.astype(single)).astype(bfloat)
+
+    waited = [grads[0, 0, 0]]
+    for local in (1, 0):
+        for by_x in range(head_count // 2):
+            grads[local, by_x, 0] = add(
+                grads[local, by_x, 0], grid.shift(grads[local, by_x, 1], "c", -1)
+            )
+    waited += [grads[1, by_x, 0] for by_x in (0, 1)]
+    for local in (1, 0):
+        for by_x in range(1, head_count // 2):
+            grads[local, 0, 0] = add(
+                grads[local, 0, 0], grid.shift(grads[local, by_x, 0], "x", -by_x)
+            )
+    grad_piece = grads[0, 0, 0].astype(single) + grid.shift(grads[1, 0, 0], "zh", -1).astype(single)
+    grad_in_own = grad_piece[: hidden // model_width * deep_in]
+    grad_in_own = grad_in_own.reshape(-1, deep_in, model_width).transpose(1, 0, 2)
+    grad_in_own = grad_in_own.reshape(1, deep_in, hidden)
+    grad_hidden_own = grad_piece[hidden // model_width * deep_in :][None]
+    output = whole_call(
+        lambda *refs: output_kernel(providers, cap, *refs),
+        shape((row_count, model_width), bfloat),
+        in_specs=[smem] + [vmem] * (2 + providers),
+        micros=8,
+    )(targets, res, slots, *out_parcels)
 
     grad_tokens, grad_w, grad_gain1, grad_gain2, grad_router = whole_call(
-        backward_kernel,
+        lambda *refs: backward_kernel(providers, cap, head_count, len(waited), *refs),
         (
             shape((row_count, model_width), single),
             shape((4, model_width, model_width), bfloat),
@@ -413,7 +935,9 @@
             shape((1, model_width), single),
             shape((padded, model_width), single),
         ),
+        in_specs=[smem] + [vmem] * 7 + [hbm] * 2 + [vmem] * (7 + providers) + [hbm] * len(waited),
         scratch=[
+            pltpu.VMEM((padded, row_count), single),
             pltpu.VMEM((row_count, model_width), single),
             pltpu.VMEM((row_count, model_width), bfloat),
             pltpu.VMEM((row_count, model_width), bfloat),
@@ -421,12 +945,14 @@
             pltpu.VMEM((row_count, model_width), single),
             pltpu.VMEM((row_count, model_width), single),
             pltpu.VMEM((row_count, model_width), bfloat),
+            pltpu.VMEM((4, model_width, model_width), bfloat),
+            pltpu.SemaphoreType.DMA((2, head_count // 2)),
         ],
-        flops=2 * 10 * row_count * model_width**2,
-        moved=24 * row_count * model_width,
+        micros=34,
     )(
-        tokens, cotangent, res, two_low, proj, attn, stat, wqkv, wot, gain1, gain2, router,
-        segc, segw, gate, inner, grad_copies,
+        targets,
+        tokens, cotangent, res, two_low, proj, attn, stat, *weights, gain1, gain2, router,
+        segc, segw, gate, slots, *grad_parcels, *waited,
     )
 
     pieces = (
@@ -444,19 +970,14 @@
     )
     packed = jnp.concatenate([pieces, smalls], axis=2)
     packed = packed.reshape(*grid.shape, 4 * deep + small_rows, wide).transpose(4, 3, 2, 1, 0, 5, 6)
+    packed = after(packed, grads[0, 0, 0], *out_parcels[1:3])
     for name in ("c", "x", "y", "zl", "zh"):
+        if name == "y":
+            packed = after(packed, grad_piece)
         packed = grid.scatter_sum(packed, name)
     pieces = packed[: 4 * deep].reshape(4, deep, wide).astype(single)
     smalls = packed[4 * deep :].reshape(-1)[: (2 + expert_count) * deep].astype(single)
     smalls = smalls.reshape(2 + expert_count, deep)
-    expert_totals = (
-        lax.psum_scatter(
-            grad_in_local[None].astype(jnp.bfloat16), "head", scatter_dimension=1, tiled=True
-        ).astype(jnp.float32),
-        lax.psum_scatter(
-            grad_hidden_local[None].astype(jnp.bfloat16), "head", scatter_dimension=1, tiled=True
-        ).astype(jnp.float32),
-    )
     return (
         output,
         grad_tokens,
@@ -465,8 +986,8 @@
         smalls[0],
         smalls[1],
         smalls[2:].T,
-        expert_totals[0],
-        expert_totals[1],
+        grad_in_own,
+        grad_hidden_own,
     )
 
 

time: 676 us -> 396 us (0.59)
  waiting for transfers between devices: 293 us -> 131 us
  Pallas kernels: 48.3 us -> 185 us
  matrix products: 114 us -> 0 us
  local copies, waits for them, and re-layouts: 110 us -> 30 us
  other arithmetic: 53.1 us -> 18.7 us
  between operations: 15 us -> 1.78 us
  starting transfers between devices: 33.1 us -> 25.5 us
    all_to_all x4 -> x0, waiting for transfers between devices: 229 us -> none  [the longest x1 78.7 us: per_device(): lax.all_to_all(grad_rows.reshape(expert_count, cap, model_width), 'expert...]
    pallas_call x2 -> x8, Pallas kernels: 48.3 us -> 185 us  [the longest x2 68.9 us: per_device(): whole_call(lambda *refs, count=count, new=not saved: expert_kernel(count,...]
    dot_general x6 -> x0, matrix products: 114 us -> none  [the longest x1 32.1 us: per_device(): jnp.einsum('rd,fd->rf', flat_grad, expert_hidden, preferred_element_type=...]
    ppermute x10 -> x36, waiting for transfers between devices: 38 us -> 131 us  [send(): return lax.ppermute(value, ('expert', 'head'), pairs)]
    gather x5 -> x1, local copies, waits for them, and re-layouts: 28.1 us -> 0.64 us  [meta_of(): return jnp.concatenate([experts, kept[experts], names['c'][None]])]
    all_gather x2 -> x0, waiting for transfers between devices: 25.3 us -> none  [the longest x1 25 us: per_device(): lax.all_gather(weight_in.astype(bfloat), 'head', axis=1, tiled=True)[0]]
    reduce_sum x5 -> x1, other arithmetic: 20.1 us -> 0.04 us  [per_device(): half_tiles = jnp.sum((numbers + HALF - 1) // HALF, axis=1)]
    all_to_all x4 -> x0, starting transfers between devices: 18.6 us -> none  [the longest x1 4.7 us: per_device(): lax.all_to_all(grad_rows.reshape(expert_count, cap, model_width), 'expert...]
  transfers between devices with their start and end apart: 18 -> 36, of which waited for: 14 -> 13; matrix products, arithmetic and copies ran while one was open for 28% -> 9% of each run, Pallas kernels for 4% -> 47%
where the time goes in v2:
time: 396 us; the launch traced here: 392 us
  Pallas kernels  185 us (47%)
  waiting for transfers between devices  131 us (33%)
  local copies, waits for them, and re-layouts  30 us (8%)
  starting transfers between devices  25.5 us (6%)
  other arithmetic  18.7 us (5%)
    ppermute x36, waiting for transfers between devices, send(): return lax.ppermute(value, ('expert', 'head'), pairs)  131 us
    pallas_call x2, Pallas kernels, per_device(): whole_call(lambda *refs, count=count, new=not saved: expert_kernel(count,...  68.9 us
    pallas_call x1, Pallas kernels, per_device(): whole_call(lambda *refs: backward_kernel(providers, cap, head_count, len(...  35.8 us
    pallas_call x1, Pallas kernels, per_device(): whole_call(lambda *refs: weight_kernel(head_count, *refs), [piece] * len(...  28.9 us
    pallas_call x1, Pallas kernels, per_device(): whole_call(lambda *refs: forward_kernel(cap, head_count, *refs), [shape((...  28.8 us
    ppermute x36, starting transfers between devices, send(): return lax.ppermute(value, ('expert', 'head'), pairs)  25.5 us
    pallas_call x1, Pallas kernels, per_device(): whole_call(lambda *refs: cotangent_kernel(cap, *refs), [parcel] * provide...  11.2 us
    pallas_call x1, Pallas kernels, per_device(): whole_call(lambda *refs: output_kernel(providers, cap, *refs), shape((row...  8.37 us
  transfers between devices with their start and end apart: 36, of which 13 were waited for; matrix products, arithmetic and copies ran while one was open for 9% of the time, Pallas kernels for 47%

profile of v2, /device:TPU:0, one launch (start us, length us, event | category | flops | bytes accessed | tf_op | source)
XLA Modules:
  0.0 392.1 jit_solution(17137182614287248946)
XLA Ops:
  2.1 0.8 convert_bitcast_fusion
  2.9 0.9 convert.54
  3.8 4.1 %collective-permute-start = (bf16[261,128]{1,0:T(8,128)(2,1)S(1)}, bf16[261,128]{1,0:T(8,128)(2,1)S(1)}, u32[]{:S(2)}, u32[]{:S(2)}) collective-permute-start(bf16[261,128]{1,0:T(8,128)(2,1)S(1)} %get-tuple-element.161), channel_id=1, source_target_pairs={{0,16},{1,17},{2,18},{3,19},{4,20},{5,21},{6,22},{7,23},{8,24},{9,... | collective-permute-start | bytes 200456 | tf_op jit(solution)/shard_map/ppermute | solution.py:657
  8.6 1.3 dynamic_slice.3
  10.5 3.5 shard_map.187
  14.1 1.6 collective-permute-start.1
  15.7 3.4 collective-permute-done.1
  19.2 1.6 collective-permute-start.2
  20.8 0.8 slice_reduce_fusion
  21.6 1.0 copy.61.refs_7_.refs_13_
  22.7 3.3 collective-permute-done.2
  26.3 1.6 collective-permute-start.3
  32.7 5.0 %collective-permute-done.3 = bf16[2,2,2,256,128]{4,3,2,1,0:T(8,128)(2,1)S(1)} collective-permute-done((bf16[2,2,2,256,128]{4,3,2,1,0:T(8,128)(2,1)S(1)}, bf16[2,2,2,256,128]{4,3,2,1,0:T(8,128)(2,1)S(1)}, u32[]{:S(2)}, u32[]{:S(2)}) %collective-permute-start.3) | collective-permute-done | bytes 524320 | tf_op jit(solution)/shard_map/ppermute | solution.py:657
  37.9 1.1 copy.58
  39.9 11.2 %shard_map.189 = (bf16[1040,512]{1,0:T(8,128)(2,1)}, bf16[1040,512]{1,0:T(8,128)(2,1)}, bf16[1040,512]{1,0:T(8,128)(2,1)}, bf16[1040,512]{1,0:T(8,128)(2,1)}) custom-call(s32[17]{0:T(128)} %concatenate.108.refs_0_, bf16[1024,512]{1,0:T(8,128)(2,1)} %refs_2_.1, f32[16,1024]{1,0:T(8,128)} %get-tuple-element.81.refs_11_.refs_2_.refs_16_, ...), custom_call_target="tpu_custom_call" | custom-call | flops 11530000384 | tf_op jit(solution)/shard_map/pallas_call | solution.py:777
  51.8 3.0 collective-permute-start.5
  55.7 28.8 %shard_map.188 = (bf16[3,1024,512]{2,1,0:T(8,128)(2,1)}, bf16[1024,512]{1,0:T(8,128)(2,1)}, f32[1024,512]{1,0:T(8,128)}, bf16[1024,512]{1,0:T(8,128)(2,1)}, f32[...) custom-call(s32[17]{0:T(128)} %concatenate.108.refs_0_, ...), custom_call_target="tpu_custom_call" | custom-call | flops 32284000256 | tf_op jit(solution)/shard_map/pallas_call | solution.py:783
  84.7 18.3 %collective-permute-done.15.refs_5_ = bf16[1040,512]{1,0:T(8,128)(2,1)S(1)} collective-permute-done((bf16[1040,512]{1,0:T(8,128)(2,1)}, bf16[1040,512]{1,0:T(8,128)(2,1)S(1)}, u32[]{:S(2)}, u32[]{:S(2)}) %collective-permute-start.15) | collective-permute-done | bytes 1064992 | tf_op jit(solution)/shard_map/ppermute | solution.py:657
  104.3 0.8 convert_reduce_fusion.3
  105.6 16.0 %collective-permute-done.14.refs_4_ = bf16[1040,512]{1,0:T(8,128)(2,1)} collective-permute-done((bf16[1040,512]{1,0:T(8,128)(2,1)}, bf16[1040,512]{1,0:T(8,128)(2,1)}, u32[]{:S(2)}, u32[]{:S(2)}) %collective-permute-start.14) | collective-permute-done | bytes 1064992 | tf_op jit(solution)/shard_map/ppermute | solution.py:657
  122.2 22.7 %collective-permute-done.6.refs_3_ = bf16[1024,512]{1,0:T(8,128)(2,1)} collective-permute-done((bf16[1024,512]{1,0:T(8,128)(2,1)}, bf16[1024,512]{1,0:T(8,128)(2,1)}, u32[]{:S(2)}, u32[]{:S(2)}) %collective-permute-start.6) | collective-permute-done | bytes 1048608 | tf_op jit(solution)/shard_map/ppermute | solution.py:657
  145.0 0.8 convert_reduce_fusion.1
  149.0 34.7 %shard_map.190 = (bf16[2,2048,512]{2,1,0:T(8,128)(2,1)}, bf16[2,2048,512]{2,1,0:T(8,128)(2,1)}, bf16[2,2048,2048]{2,1,0:T(8,128)(2,1)}, bf16[2,2048,2048]{2,1,0:...) custom-call(s32[10]{0:T(128)} %concatenate.112.refs_0_, ...), custom_call_target="tpu_custom_call" | custom-call | flops 28824999936 | tf_op jit(solution)/shard_map/pallas_call | solution.py:845
  183.8 1.0 copy-done.17
  184.8 34.2 %shard_map.191 = (bf16[2,2048,512]{2,1,0:T(8,128)(2,1)}, bf16[2,2048,512]{2,1,0:T(8,128)(2,1)}, bf16[2,2048,2048]{2,1,0:T(8,128)(2,1)}, bf16[2,2048,2048]{2,1,0:...) custom-call(s32[10]{0:T(128)} %concatenate.113.refs_0_, ...), custom_call_target="tpu_custom_call", output_to_operand_aliasing={{0}: (14, {}), {1}: (15, {}), {2}: (16, {}), {3}: (17, {})} | custom-call | flops 28824999936 | tf_op jit(solution)/shard_map/pallas_call | solution.py:845
  219.2 28.9 %shard_map.193 = (bf16[1024,512]{1,0:T(8,128)(2,1)}, bf16[1024,512]{1,0:T(8,128)(2,1)}, bf16[1024,512]{1,0:T(8,128)(2,1)}, bf16[1024,512]{1,0:T(8,128)(2,1)}, bf...) custom-call(s32[4]{0:T(128)} %pad_add_fusion.2.refs_0_, ...), custom_call_target="tpu_custom_call" | custom-call | flops 27672000512 | tf_op jit(solution)/shard_map/pallas_call | solution.py:883
  248.8 2.3 collective-permute-done.25
  251.1 1.5 add_convert_fusion.4.refs_23_
  252.9 1.2 collective-permute-done.27
  254.1 1.0 copy-done.3
  255.2 1.8 add_convert_fusion.2
  257.7 21.2 %collective-permute-done.31 = bf16[1024,512]{1,0:T(8,128)(2,1)} collective-permute-done((bf16[1024,512]{1,0:T(8,128)(2,1)S(1)}, bf16[1024,512]{1,0:T(8,128)(2,1)}, u32[]{:S(2)}, u32[]{:S(2)}) %collective-permute-start.31) | collective-permute-done | bytes 1048608 | tf_op jit(solution)/shard_map/ppermute | solution.py:657
  278.9 3.4 add_convert_fusion
  282.3 7.6 %collective-permute-start.32 = (bf16[1024,512]{1,0:T(8,128)(2,1)}, bf16[1024,512]{1,0:T(8,128)(2,1)}, u32[]{:S(2)}, u32[]{:S(2)}) collective-permute-start(bf16[1024,512]{1,0:T(8,128)(2,1)} %get-tuple-element.151), channel_id=1, source_target_pairs={{0,16},{1,17},{2,18},{3,19},{4,20},{5,21},{6,22},{7,23},{8,24},{9,... | collective-permute-start | bytes 3145736 | tf_op jit(solution)/shard_map/ppermute | solution.py:657
  289.8 35.8 %shard_map.194 = (f32[1024,512]{1,0:T(8,128)}, bf16[4,512,512]{2,1,0:T(8,128)(2,1)}, f32[1,512]{1,0:T(1,128)}, f32[1,512]{1,0:T(1,128)}, f32[16,512]{1,0:T(8,128)}) custom-call(s32[17]{0:T(128)} %concatenate.108.refs_0_, bf16[1024,512]{1,0:T(8,128)(2,1)} %refs_1_.5, bf16[1024,512]{1,0:T(8,128)(2,1)} %refs_2_.1, ...), custom_call_target="tpu_custom_call" | custom-call | flops 39202000896 | tf_op jit(solution)/shard_map/pallas_call | solution.py:929
  327.2 0.7 slice.278
  328.1 2.5 reshape.655
  331.5 1.0 copy-done.5
  332.5 2.4 convert_add_fusion.1
  335.1 1.1 copy.69
  336.2 2.7 collective-permute-done.29
  340.6 13.5 %collective-permute-done.30 = bf16[2,2,2,261,128]{4,2,3,1,0:T(2,128)(2,1)S(1)} collective-permute-done((bf16[2,2,2,261,128]{4,2,3,1,0:T(2,128)(2,1)S(1)}, bf16[2,2,2,261,128]{4,2,3,1,0:T(2,128)(2,1)S(1)}, u32[]{:S(2)}, u32[]{:S(2)}) %collective-permute-start.30) | collective-permute-done | bytes 534560 | tf_op jit(solution)/shard_map/ppermute | solution.py:657
  354.4 18.4 %collective-permute-done.33 = bf16[2,2,261,128]{3,2,0,1:T(8,128)(2,1)S(1)} collective-permute-done((bf16[2,2,261,128]{3,2,0,1:T(8,128)(2,1)S(1)}, bf16[2,2,261,128]{3,2,0,1:T(8,128)(2,1)S(1)}, u32[]{:S(2)}, u32[]{:S(2)}) %collective-permute-start.33) | collective-permute-done | bytes 267296 | tf_op jit(solution)/shard_map/ppermute | solution.py:657
  373.0 1.0 copy-done.14
  374.0 8.4 %shard_map.192 = bf16[1024,512]{1,0:T(8,128)(2,1)} custom-call(s32[17]{0:T(128)} %concatenate.108.refs_0_, f32[1024,512]{1,0:T(8,128)} %get-tuple-element.82.refs_1_.refs_3_, f32[16,1024]{1,0:T(8,128)} %get-tuple-element.81.refs_11_.refs_2_.refs_16_, bf16[1040,512]{1,0:T(8,128)(2,1)} %get-tuple-element.95.refs_3_, ...), custom_call_target="tpu_custom_call" | custom-call | flops 9223999488 | tf_op jit(solution)/shard_map/pallas_call | solution.py:922
  382.8 1.1 slice_bitcast_fusion
  384.7 1.7 reshape.657
  386.3 2.8 collective-permute-done.35
  (178 shorter events, 27.1 us)
Async XLA Ops:
  3.8 10.2 %collective-permute-start = (bf16[261,128]{1,0:T(8,128)(2,1)S(1)}, bf16[261,128]{1,0:T(8,128)(2,1)S(1)}, u32[]{:S(2)}, u32[]{:S(2)}) collective-permute-start(bf16[261,128]{1,0:T(8,128)(2,1)S(1)} %get-tuple-element.161), channel_id=1, source_target_pairs={{0,16},{1,17},{2,18},{3,19},{4,20},{5,21},{6,22},{7,23},{8,24},{9,... | collective-permute-start | bytes 200456 | tf_op jit(solution)/shard_map/ppermute | solution.py:657
  10.5 11.2 %copy-start.6 = (s32[1024]{0:T(1024)S(1)}, s32[1024]{0:T(1024)}, u32[]{:S(2)}) copy-start(s32[1024]{0:T(1024)} %dynamic_slice.3) | copy-start | bytes 12292
  14.1 5.1 %collective-permute-start.1 = (bf16[2,261,128]{2,1,0:T(8,128)(2,1)S(1)}, bf16[2,261,128]{2,1,0:T(8,128)(2,1)S(1)}, u32[]{:S(2)}, u32[]{:S(2)}) collective-permute-start(bf16[2,261,128]{2,1,0:T(8,128)(2,1)S(1)} %maximum_select_fusion.5), channel_id=1, source_target_pairs={{0,8},{1,9},{2,10},{3,11},{4,12},{5,13},{6,14},{7,15},{8,0},{9,1},... | collective-permute-start | bytes 400904 | tf_op jit(solution)/shard_map/ppermute | solution.py:657
  19.2 6.8 %collective-permute-start.2 = (bf16[2,2,261,128]{3,2,1,0:T(8,128)(2,1)S(1)}, bf16[2,2,261,128]{3,2,1,0:T(8,128)(2,1)S(1)}, u32[]{:S(2)}, u32[]{:S(2)}) collective-permute-start(bf16[2,2,261,128]{3,2,1,0:T(8,128)(2,1)S(1)} %maximum_select_fusion.3), channel_id=1, source_target_pairs={{0,4},{1,5},{2,6},{3,7},{4,0},{5,1},{6,2},{7,3},{8,12},{9,13},{10,... | collective-permute-start | bytes 801800 | tf_op jit(solution)/shard_map/ppermute | solution.py:657
  26.1 4.3 %copy-start = (bf16[2,2,2,261,128]{4,3,2,1,0:T(8,128)(2,1)}, bf16[2,2,2,261,128]{4,3,2,1,0:T(8,128)(2,1)S(1)}, u32[]{:S(2)}) copy-start(bf16[2,2,2,261,128]{4,3,2,1,0:T(8,128)(2,1)S(1)} %maximum_select_fusion.1.refs_4_) | copy-start | bytes 1603588
  26.3 11.3 %collective-permute-start.3 = (bf16[2,2,2,256,128]{4,3,2,1,0:T(8,128)(2,1)S(1)}, bf16[2,2,2,256,128]{4,3,2,1,0:T(8,128)(2,1)S(1)}, u32[]{:S(2)}, u32[]{:S(2)}) collective-permute-start(bf16[2,2,2,256,128]{4,3,2,1,0:T(8,128)(2,1)S(1)} %get-tuple-element.158), channel_id=1, source_target_pairs={{0,2},{1,3},{2,0},{3,1},{4,6},{5,7},{6,4},{7,5},{8,10},{9,11},{10,... | collective-permute-start | bytes 1572872 | tf_op jit(solution)/shard_map/ppermute | solution.py:657
  29.9 54.6 %collective-permute-start.10 = (bf16[1024,512]{1,0:T(8,128)(2,1)}, bf16[1024,512]{1,0:T(8,128)(2,1)}, u32[]{:S(2)}, u32[]{:S(2)}) collective-permute-start(bf16[1024,512]{1,0:T(8,128)(2,1)} %get-tuple-element.92.refs_6_), channel_id=1, source_target_pairs={{0,16},{1,17},{2,18},{3,19},{4,20},{5,21},{6,22},{7,23},{8,24},{9,... | collective-permute-start | bytes 3145736 | tf_op jit(solution)/shard_map/ppermute | solution.py:657
  39.8 11.3 %copy-start.4 = (bf16[4,512,256]{2,1,0:T(8,128)(2,1)}, bf16[4,512,256]{2,1,0:T(8,128)(2,1)S(1)}, u32[]{:S(2)}) copy-start(bf16[4,512,256]{2,1,0:T(8,128)(2,1)S(1)} %reshape.650.refs_2_.refs_8_) | copy-start | bytes 3145732
  39.8 15.0 %collective-permute-start.4 = (bf16[4,512,256]{2,1,0:T(8,128)(2,1)S(1)}, bf16[4,512,256]{2,1,0:T(8,128)(2,1)S(1)}, u32[]{:S(2)}, u32[]{:S(2)}) collective-permute-start(bf16[4,512,256]{2,1,0:T(8,128)(2,1)S(1)} %reshape.650.refs_2_.refs_8_), channel_id=1, source_target_pairs={{0,1},{1,0},{2,3},{3,2},{4,5},{5,4},{6,7},{7,6},{8,9},{9,8},{10,11... | collective-permute-start | bytes 3145736 | tf_op jit(solution)/shard_map/ppermute | solution.py:657
  39.8 11.2 %copy-start.15 = (bf16[1024,512]{1,0:T(8,128)(2,1)S(1)}, bf16[1024,512]{1,0:T(8,128)(2,1)}, u32[]{:S(2)}) copy-start(bf16[1024,512]{1,0:T(8,128)(2,1)} %get-tuple-element.92.refs_6_) | copy-start | bytes 3145732
  51.1 54.5 %collective-permute-start.8 = (bf16[1024,512]{1,0:T(8,128)(2,1)S(1)}, bf16[1024,512]{1,0:T(8,128)(2,1)}, u32[]{:S(2)}, u32[]{:S(2)}) collective-permute-start(bf16[1024,512]{1,0:T(8,128)(2,1)S(1)} %copy-done.15), channel_id=1, source_target_pairs={{0,2},{1,3},{2,0},{3,1},{4,6},{5,7},{6,4},{7,5},{8,10},{9,11},{10,... | collective-permute-start | bytes 3145736 | tf_op jit(solution)/shard_map/ppermute | solution.py:657
  51.8 69.8 %collective-permute-start.5 = (bf16[1040,512]{1,0:T(8,128)(2,1)}, bf16[1040,512]{1,0:T(8,128)(2,1)S(1)}, u32[]{:S(2)}, u32[]{:S(2)}) collective-permute-start(bf16[1040,512]{1,0:T(8,128)(2,1)} %get-tuple-element.85), channel_id=1, source_target_pairs={{0,12},{1,13},{2,14},{3,15},{4,8},{5,9},{6,10},{7,11},{8,4},{9,5},... | collective-permute-start | bytes 3194888 | tf_op jit(solution)/shard_map/ppermute | solution.py:657
  54.7 66.8 %collective-permute-start.14 = (bf16[1040,512]{1,0:T(8,128)(2,1)}, bf16[1040,512]{1,0:T(8,128)(2,1)}, u32[]{:S(2)}, u32[]{:S(2)}) collective-permute-start(bf16[1040,512]{1,0:T(8,128)(2,1)} %get-tuple-element.96), channel_id=1, source_target_pairs={{0,8},{1,9},{2,10},{3,11},{4,12},{5,13},{6,14},{7,15},{8,0},{9,1},... | collective-permute-start | bytes 3194888 | tf_op jit(solution)/shard_map/ppermute | solution.py:657
  54.8 48.2 %collective-permute-start.15 = (bf16[1040,512]{1,0:T(8,128)(2,1)}, bf16[1040,512]{1,0:T(8,128)(2,1)S(1)}, u32[]{:S(2)}, u32[]{:S(2)}) collective-permute-start(bf16[1040,512]{1,0:T(8,128)(2,1)} %get-tuple-element.98), channel_id=1, source_target_pairs={{0,4},{1,5},{2,6},{3,7},{4,0},{5,1},{6,2},{7,3},{8,12},{9,13},{10,... | collective-permute-start | bytes 3194888 | tf_op jit(solution)/shard_map/ppermute | solution.py:657
  55.7 47.9 %copy-start.7 = (bf16[16,512]{1,0:T(8,128)(2,1)S(1)}, bf16[16,512]{1,0:T(8,128)(2,1)}, u32[]{:S(2)}) copy-start(bf16[16,512]{1,0:T(8,128)(2,1)} %pad.14.refs_6_.refs_12_) | copy-start | bytes 49156
  84.5 37.7 %collective-permute-start.12 = (bf16[1024,512]{1,0:T(8,128)(2,1)}, bf16[1024,512]{1,0:T(8,128)(2,1)}, u32[]{:S(2)}, u32[]{:S(2)}) collective-permute-start(bf16[1024,512]{1,0:T(8,128)(2,1)} %collective-permute-done.10.refs_10_), channel_id=1, source_target_pairs={{0,2},{1,3},{2,0},{3,1},{4,6},{5,7},{6,4},{7,5},{8,10},{9,11},{10,... | collective-permute-start | bytes 3145736 | tf_op jit(solution)/shard_map/ppermute | solution.py:657
  103.0 80.7 %copy-start.9 = (bf16[1040,512]{1,0:T(8,128)(2,1)}, bf16[1040,512]{1,0:T(8,128)(2,1)S(1)}, u32[]{:S(2)}) copy-start(bf16[1040,512]{1,0:T(8,128)(2,1)S(1)} %collective-permute-done.15.refs_5_) | copy-start | bytes 3194884
  103.0 42.0 %collective-permute-start.6 = (bf16[1024,512]{1,0:T(8,128)(2,1)}, bf16[1024,512]{1,0:T(8,128)(2,1)}, u32[]{:S(2)}, u32[]{:S(2)}) collective-permute-start(bf16[1024,512]{1,0:T(8,128)(2,1)} %get-tuple-element.89), channel_id=1, source_target_pairs={{0,12},{1,13},{2,14},{3,15},{4,8},{5,9},{6,10},{7,11},{8,4},{9,5},... | collective-permute-start | bytes 3145736 | tf_op jit(solution)/shard_map/ppermute | solution.py:657
  105.6 42.9 %collective-permute-start.7 = (bf16[1024,512]{1,0:T(8,128)(2,1)S(1)}, bf16[1024,512]{1,0:T(8,128)(2,1)}, u32[]{:S(2)}, u32[]{:S(2)}) collective-permute-start(bf16[1024,512]{1,0:T(8,128)(2,1)S(1)} %copy-done.15), channel_id=1, source_target_pairs={{0,1},{1,0},{2,3},{3,2},{4,5},{5,4},{6,7},{7,6},{8,9},{9,8},{10,11... | collective-permute-start | bytes 3145736 | tf_op jit(solution)/shard_map/ppermute | solution.py:657
  121.6 27.4 %collective-permute-start.9 = (bf16[1024,512]{1,0:T(8,128)(2,1)}, bf16[1024,512]{1,0:T(8,128)(2,1)}, u32[]{:S(2)}, u32[]{:S(2)}) collective-permute-start(bf16[1024,512]{1,0:T(8,128)(2,1)} %collective-permute-done.8.refs_8_), channel_id=1, source_target_pairs={{0,1},{1,0},{2,3},{3,2},{4,5},{5,4},{6,7},{7,6},{8,9},{9,8},{10,11... | collective-permute-start | bytes 3145736 | tf_op jit(solution)/shard_map/ppermute | solution.py:657
  121.6 27.4 %copy-start.10 = (bf16[1040,512]{1,0:T(8,128)(2,1)}, bf16[1040,512]{1,0:T(8,128)(2,1)S(1)}, u32[]{:S(2)}) copy-start(bf16[1040,512]{1,0:T(8,128)(2,1)S(1)} %collective-permute-done.5.refs_5_) | copy-start | bytes 3194884
  121.6 27.4 %collective-permute-start.11 = (bf16[1024,512]{1,0:T(8,128)(2,1)}, bf16[1024,512]{1,0:T(8,128)(2,1)}, u32[]{:S(2)}, u32[]{:S(2)}) collective-permute-start(bf16[1024,512]{1,0:T(8,128)(2,1)} %collective-permute-done.10.refs_10_), channel_id=1, source_target_pairs={{0,1},{1,0},{2,3},{3,2},{4,5},{5,4},{6,7},{7,6},{8,9},{9,8},{10,11... | collective-permute-start | bytes 3145736 | tf_op jit(solution)/shard_map/ppermute | solution.py:657
  145.0 4.0 %collective-permute-start.13 = (bf16[1024,512]{1,0:T(8,128)(2,1)}, bf16[1024,512]{1,0:T(8,128)(2,1)}, u32[]{:S(2)}, u32[]{:S(2)}) collective-permute-start(bf16[1024,512]{1,0:T(8,128)(2,1)} %collective-permute-done.12.refs_12_), channel_id=1, source_target_pairs={{0,1},{1,0},{2,3},{3,2},{4,5},{5,4},{6,7},{7,6},{8,9},{9,8},{10,11... | collective-permute-start | bytes 3145736 | tf_op jit(solution)/shard_map/ppermute | solution.py:657
  146.6 37.2 %collective-permute-start.16 = (bf16[1024,512]{1,0:T(8,128)(2,1)}, bf16[1024,512]{1,0:T(8,128)(2,1)}, u32[]{:S(2)}, u32[]{:S(2)}) collective-permute-start(bf16[1024,512]{1,0:T(8,128)(2,1)} %get-tuple-element.100), channel_id=1, source_target_pairs={{0,8},{1,9},{2,10},{3,11},{4,12},{5,13},{6,14},{7,15},{8,0},{9,1},... | collective-permute-start | bytes 3145736 | tf_op jit(solution)/shard_map/ppermute | solution.py:657
  148.5 35.3 %collective-permute-start.17 = (bf16[1024,512]{1,0:T(8,128)(2,1)}, bf16[1024,512]{1,0:T(8,128)(2,1)S(1)}, u32[]{:S(2)}, u32[]{:S(2)}) collective-permute-start(bf16[1024,512]{1,0:T(8,128)(2,1)} %get-tuple-element.101), channel_id=1, source_target_pairs={{0,4},{1,5},{2,6},{3,7},{4,0},{5,1},{6,2},{7,3},{8,12},{9,13},{10,... | collective-permute-start | bytes 3145736 | tf_op jit(solution)/shard_map/ppermute | solution.py:657
  183.7 64.4 %collective-permute-start.23 = (bf16[1040,512]{1,0:T(8,128)(2,1)}, bf16[1040,512]{1,0:T(8,128)(2,1)S(1)}, u32[]{:S(2)}, u32[]{:S(2)}) collective-permute-start(bf16[1040,512]{1,0:T(8,128)(2,1)} %get-tuple-element.128), channel_id=1, source_target_pairs={{0,12},{1,13},{2,14},{3,15},{4,8},{5,9},{6,10},{7,11},{8,4},{9,5},... | collective-permute-start | bytes 3194888 | tf_op jit(solution)/shard_map/ppermute | solution.py:657
  219.1 29.0 %collective-permute-start.21 = (bf16[1040,512]{1,0:T(8,128)(2,1)}, bf16[1040,512]{1,0:T(8,128)(2,1)S(1)}, u32[]{:S(2)}, u32[]{:S(2)}) collective-permute-start(bf16[1040,512]{1,0:T(8,128)(2,1)} %get-tuple-element.126), channel_id=1, source_target_pairs={{0,4},{1,5},{2,6},{3,7},{4,0},{5,1},{6,2},{7,3},{8,12},{9,13},{10,... | collective-permute-start | bytes 3194888 | tf_op jit(solution)/shard_map/ppermute | solution.py:657
  219.2 29.0 %collective-permute-start.22 = (bf16[1040,512]{1,0:T(8,128)(2,1)}, bf16[1040,512]{1,0:T(8,128)(2,1)S(1)}, u32[]{:S(2)}, u32[]{:S(2)}) collective-permute-start(bf16[1040,512]{1,0:T(8,128)(2,1)} %get-tuple-element.127), channel_id=1, source_target_pairs={{0,8},{1,9},{2,10},{3,11},{4,12},{5,13},{6,14},{7,15},{8,0},{9,1},... | collective-permute-start | bytes 3194888 | tf_op jit(solution)/shard_map/ppermute | solution.py:657
  248.1 4.5 %copy-start.11 = (bf16[1040,512]{1,0:T(8,128)(2,1)}, bf16[1040,512]{1,0:T(8,128)(2,1)S(1)}, u32[]{:S(2)}) copy-start(bf16[1040,512]{1,0:T(8,128)(2,1)S(1)} %collective-permute-done.23.refs_20_) | copy-start | bytes 3194884
  248.1 4.5 %copy-start.12 = (bf16[1040,512]{1,0:T(8,128)(2,1)}, bf16[1040,512]{1,0:T(8,128)(2,1)S(1)}, u32[]{:S(2)}) copy-start(bf16[1040,512]{1,0:T(8,128)(2,1)S(1)} %collective-permute-done.21.refs_18_) | copy-start | bytes 3194884
  248.2 4.5 %copy-start.13 = (bf16[1040,512]{1,0:T(8,128)(2,1)}, bf16[1040,512]{1,0:T(8,128)(2,1)S(1)}, u32[]{:S(2)}) copy-start(bf16[1040,512]{1,0:T(8,128)(2,1)S(1)} %collective-permute-done.22.refs_19_) | copy-start | bytes 3194884
  248.2 2.9 collective-permute-start.25
  248.2 5.9 %collective-permute-start.27 = (bf16[1024,512]{1,0:T(8,128)(2,1)}, bf16[1024,512]{1,0:T(8,128)(2,1)S(1)}, u32[]{:S(2)}, u32[]{:S(2)}) collective-permute-start(bf16[1024,512]{1,0:T(8,128)(2,1)} %get-tuple-element.144), channel_id=1, source_target_pairs={{0,1},{1,0},{2,3},{3,2},{4,5},{5,4},{6,7},{7,6},{8,9},{9,8},{10,11... | collective-permute-start | bytes 3145736 | tf_op jit(solution)/shard_map/ppermute | solution.py:657
  248.7 8.3 %collective-permute-start.24 = (bf16[1024,512]{1,0:T(8,128)(2,1)}, bf16[1024,512]{1,0:T(8,128)(2,1)}, u32[]{:S(2)}, u32[]{:S(2)}) collective-permute-start(bf16[1024,512]{1,0:T(8,128)(2,1)} %get-tuple-element.134), channel_id=1, source_target_pairs={{0,1},{1,0},{2,3},{3,2},{4,5},{5,4},{6,7},{7,6},{8,9},{9,8},{10,11... | collective-permute-start | bytes 3145736 | tf_op jit(solution)/shard_map/ppermute | solution.py:657
  252.7 29.6 %copy-start.2 = (bf16[1024,512]{1,0:T(8,128)(2,1)}, bf16[1024,512]{1,0:T(8,128)(2,1)S(1)}, u32[]{:S(2)}) copy-start(bf16[1024,512]{1,0:T(8,128)(2,1)S(1)} %add_convert_fusion.4.refs_23_) | copy-start | bytes 3145732
  252.7 26.2 %copy-start.1 = (bf16[1024,512]{1,0:T(8,128)(2,1)S(1)}, bf16[1024,512]{1,0:T(8,128)(2,1)}, u32[]{:S(2)}) copy-start(bf16[1024,512]{1,0:T(8,128)(2,1)} %get-tuple-element.133) | copy-start | bytes 3145732
  252.7 26.2 %collective-permute-start.31 = (bf16[1024,512]{1,0:T(8,128)(2,1)S(1)}, bf16[1024,512]{1,0:T(8,128)(2,1)}, u32[]{:S(2)}, u32[]{:S(2)}) collective-permute-start(bf16[1024,512]{1,0:T(8,128)(2,1)S(1)} %add_convert_fusion.4.refs_23_), channel_id=1, source_target_pairs={{0,2},{1,3},{2,0},{3,1},{4,6},{5,7},{6,4},{7,5},{8,10},{9,11},{10,... | collective-permute-start | bytes 3145736 | tf_op jit(solution)/shard_map/ppermute | solution.py:657
  252.8 82.1 %collective-permute-start.18 = (bf16[1040,512]{1,0:T(8,128)(2,1)}, bf16[1040,512]{1,0:T(8,128)(2,1)}, u32[]{:S(2)}, u32[]{:S(2)}) collective-permute-start(bf16[1040,512]{1,0:T(8,128)(2,1)} %get-tuple-element.106), channel_id=1, source_target_pairs={{0,4},{1,5},{2,6},{3,7},{4,0},{5,1},{6,2},{7,3},{8,12},{9,13},{10,... | collective-permute-start | bytes 3194888 | tf_op jit(solution)/shard_map/ppermute | solution.py:657
  252.8 82.1 %collective-permute-start.19 = (bf16[1040,512]{1,0:T(8,128)(2,1)}, bf16[1040,512]{1,0:T(8,128)(2,1)}, u32[]{:S(2)}, u32[]{:S(2)}) collective-permute-start(bf16[1040,512]{1,0:T(8,128)(2,1)} %get-tuple-element.107), channel_id=1, source_target_pairs={{0,8},{1,9},{2,10},{3,11},{4,12},{5,13},{6,14},{7,15},{8,0},{9,1},... | collective-permute-start | bytes 3194888 | tf_op jit(solution)/shard_map/ppermute | solution.py:657
  255.1 76.4 %collective-permute-start.26 = (bf16[1024,512]{1,0:T(8,128)(2,1)}, bf16[1024,512]{1,0:T(8,128)(2,1)}, u32[]{:S(2)}, u32[]{:S(2)}) collective-permute-start(bf16[1024,512]{1,0:T(8,128)(2,1)} %get-tuple-element.142), channel_id=1, source_target_pairs={{0,1},{1,0},{2,3},{3,2},{4,5},{5,4},{6,7},{7,6},{8,9},{9,8},{10,11... | collective-permute-start | bytes 3145736 | tf_op jit(solution)/shard_map/ppermute | solution.py:657
  257.1 74.4 %collective-permute-start.28 = (bf16[1024,512]{1,0:T(8,128)(2,1)S(1)}, bf16[1024,512]{1,0:T(8,128)(2,1)}, u32[]{:S(2)}, u32[]{:S(2)}) collective-permute-start(bf16[1024,512]{1,0:T(8,128)(2,1)S(1)} %add_convert_fusion.2), channel_id=1, source_target_pairs={{0,2},{1,3},{2,0},{3,1},{4,6},{5,7},{6,4},{7,5},{8,10},{9,11},{10,... | collective-permute-start | bytes 3145736 | tf_op jit(solution)/shard_map/ppermute | solution.py:657
  282.3 49.2 %collective-permute-start.32 = (bf16[1024,512]{1,0:T(8,128)(2,1)}, bf16[1024,512]{1,0:T(8,128)(2,1)}, u32[]{:S(2)}, u32[]{:S(2)}) collective-permute-start(bf16[1024,512]{1,0:T(8,128)(2,1)} %get-tuple-element.151), channel_id=1, source_target_pairs={{0,16},{1,17},{2,18},{3,19},{4,20},{5,21},{6,22},{7,23},{8,24},{9,... | collective-permute-start | bytes 3145736 | tf_op jit(solution)/shard_map/ppermute | solution.py:657
  336.2 2.8 collective-permute-start.29
  339.8 14.2 %collective-permute-start.30 = (bf16[2,2,2,261,128]{4,2,3,1,0:T(2,128)(2,1)S(1)}, bf16[2,2,2,261,128]{4,2,3,1,0:T(2,128)(2,1)S(1)}, u32[]{:S(2)}, u32[]{:S(2)}) collective-permute-start(bf16[2,2,2,261,128]{4,2,3,1,0:T(2,128)(2,1)S(1)} %copy.71), channel_id=1, source_target_pairs={{0,2},{1,3},{2,0},{3,1},{4,6},{5,7},{6,4},{7,5},{8,10},{9,11},{10,... | collective-permute-start | bytes 1603592 | tf_op jit(solution)/shard_map/ppermute | solution.py:657
  340.6 32.5 %collective-permute-start.20 = (bf16[1040,512]{1,0:T(8,128)(2,1)S(1)}, bf16[1040,512]{1,0:T(8,128)(2,1)S(1)}, u32[]{:S(2)}, u32[]{:S(2)}) collective-permute-start(bf16[1040,512]{1,0:T(8,128)(2,1)S(1)} %copy-done.8), channel_id=1, source_target_pairs={{0,12},{1,13},{2,14},{3,15},{4,8},{5,9},{6,10},{7,11},{8,4},{9,5},... | collective-permute-start | bytes 3194888 | tf_op jit(solution)/shard_map/ppermute | solution.py:657
  354.4 18.4 %collective-permute-start.33 = (bf16[2,2,261,128]{3,2,0,1:T(8,128)(2,1)S(1)}, bf16[2,2,261,128]{3,2,0,1:T(8,128)(2,1)S(1)}, u32[]{:S(2)}, u32[]{:S(2)}) collective-permute-start(bf16[2,2,261,128]{3,2,0,1:T(8,128)(2,1)S(1)} %fusion.4), channel_id=1, source_target_pairs={{0,4},{1,5},{2,6},{3,7},{4,0},{5,1},{6,2},{7,3},{8,12},{9,13},{10,... | collective-permute-start | bytes 801800 | tf_op jit(solution)/shard_map/ppermute | solution.py:657
  372.9 9.4 %collective-permute-start.34 = (bf16[2,261,128]{2,1,0:T(8,128)(2,1)S(1)}, bf16[2,261,128]{2,1,0:T(8,128)(2,1)S(1)}, u32[]{:S(2)}, u32[]{:S(2)}) collective-permute-start(bf16[2,261,128]{2,1,0:T(8,128)(2,1)S(1)} %fusion.6), channel_id=1, source_target_pairs={{0,8},{1,9},{2,10},{3,11},{4,12},{5,13},{6,14},{7,15},{8,0},{9,1},... | collective-permute-start | bytes 400904 | tf_op jit(solution)/shard_map/ppermute | solution.py:657
  382.5 6.7 %collective-permute-start.35 = (bf16[261,128]{1,0:T(8,128)(2,1)S(1)}, bf16[261,128]{1,0:T(8,128)(2,1)S(1)}, u32[]{:S(2)}, u32[]{:S(2)}) collective-permute-start(bf16[261,128]{1,0:T(8,128)(2,1)S(1)} %select_bitcast_fusion.2), channel_id=1, source_target_pairs={{0,16},{1,17},{2,18},{3,19},{4,20},{5,21},{6,22},{7,23},{8,24},{9,... | collective-permute-start | bytes 200456 | tf_op jit(solution)/shard_map/ppermute | solution.py:657
  (6 other events, 6.4 us)
